TPU v7x, 256 devices: a whole 4x4x8 slice. The times are simulated.
256 devices in a mesh: seq: 64 (over z, y, x_hi), head: 4 (over x_lo, core).
Axes of the slice: x: 4 (x_hi: 2, x_lo: 2; x = x_hi * 2 + x_lo), y: 4, z: 8, core: 2. Of those that a mesh axis runs over, the one named last changes fastest.
Arguments:
- queries: bfloat16 [32768, 12, 128], P('seq', 'head'), may hold values from -130 to 130
- keys: bfloat16 [32768, 12, 128], P('seq', 'head'), may hold values from -10 to 10
- values: bfloat16 [32768, 12, 128], P('seq', 'head'), may hold values from -8 to 8
- w_out: bfloat16 [768, 768], P('head'), may hold values from -0.21875 to 0.21875
Outputs:
- mixed: bfloat16 [32768, 12, 128], P('seq', 'head')
All inputs are finite; a program needn't handle non-finite values.
Results may differ from a plain program's by a relative error of at most 0.03.
Values may be sent and summed in bfloat16 or wider, within the bound.
No kernel may reach another device: no remote copies, remote signals or barrier semaphores. Data moves between devices by JAX's collectives and lax.ppermute only.
A program may use at most 64 MiB of HBM per device.

v0:
```python
import functools
import math

import jax
import jax.numpy as jnp
from jax import lax
from jax.experimental import pallas as pl
from jax.experimental.pallas import tpu as pltpu
from jax.sharding import PartitionSpec as P

HEAD_DIM = 64
NR = 128
HALF = NR // 2
LANES = 2 * HEAD_DIM
LEVELS = 3
POOL = 1024
BF16 = jnp.bfloat16
F32 = jnp.float32
SCALE2 = HEAD_DIM ** (-0.5) * math.log2(math.e)
FAR = HALF
VMEM = 16 * 1024 * 1024
LAST = 2
HALO_ROWS = 2 * HALF + LEVELS * FAR


def low_lanes(rows):
    return lax.broadcasted_iota(jnp.int32, (rows, LANES), 1) < HEAD_DIM


def swap(x):
    return pltpu.roll(x, HEAD_DIM, 1)


def swap16(x):
    return pltpu.roll(x, HEAD_DIM, 1)


def fold_pairs(lo, hi):
    lo, hi = lo.astype(F32), hi.astype(F32)
    return jnp.where(low_lanes(lo.shape[0]), lo + swap(lo), hi + swap(hi))


def halve(scratch, x):
    rows = x.shape[0]
    scratch[pl.ds(0, rows), :] = x
    return scratch[pl.ds(0, rows // 2, 2), :] + scratch[pl.ds(1, rows // 2, 2), :]


def pooled_vk(sums, factor):
    scale = jnp.where(low_lanes(1), 1.0 / factor, factor ** (-0.5))
    return (sums * scale).astype(BF16)


def ones_high(v):
    return jnp.where(low_lanes(v.shape[0]), v, jnp.ones_like(v))


def put_pairs(keys, values, block, k, v):
    at = block * NR
    keys[at : at + HALF, :] = k
    keys[at + HALF : at + NR, :] = swap16(k)
    values[at : at + HALF, :] = ones_high(v)
    values[at + HALF : at + NR, :] = ones_high(swap16(v))


def scores_of(lhs, keys):
    return lax.dot_general(lhs, keys, (((1,), (1,)), ((), ())), preferred_element_type=F32)


def group_matrix(rows, shift):
    group = [lax.broadcasted_iota(jnp.int32, (rows, rows), axis) >> shift for axis in range(2)]
    return jnp.where(group[0] == group[1], 1.0, 0.0).astype(BF16)


def prepare_kernel(k_hbm, v_hbm, place, top, first_out, second_out, k, v, scratch, read):
    heads, rows = k.shape[0], k.shape[1]
    even = lax.rem(place[0], 2) == 0
    loads = [
        [
            pltpu.make_async_copy(source.at[head], into.at[head], read.at[head, index])
            for index, (source, into) in enumerate(((k_hbm, k), (v_hbm, v)))
        ]
        for head in range(heads)
    ]
    for pair in loads:
        for copy in pair:
            copy.start()
    for head in range(heads):
        for copy in loads[head]:
            copy.wait()
        lows, highs = [], []
        for source in (k, v):
            lows.append(source[head, 0:HALF, :])
            highs.append(source[head, rows - HALF : rows, :])
        sums = fold_pairs(v[head], k[head])
        for level in range(1, LEVELS + 1):
            if level > 1:
                sums = halve(scratch.at[head], sums)
            vk = pooled_vk(sums, 2**level)
            lows.append(vk[HALF : HALF + FAR])
            highs.append(vk[vk.shape[0] - HALF - FAR : vk.shape[0] - HALF])
        for index, (low, high) in enumerate(zip(lows, highs)):
            at = slice(index * FAR, (index + 1) * FAR)
            first_out[head, at, :] = jnp.where(even, high, low)
            second_out[head, at, :] = jnp.where(even, low, high)
        top[:, head, :] = jnp.broadcast_to(pooled_vk(jnp.sum(sums, axis=0, keepdims=True), POOL), (top.shape[0], LANES))


def cut_kernel(w_ref, me, *outs):
    half, width = outs[0].shape[1], w_ref.shape[1] // me.shape[1]
    for index in range(me.shape[1]):

        @pl.when(me[0, 0] == index)
        def _(index=index):
            for slot, out in enumerate(outs):
                for core in range(2):
                    at = (index ^ (2 * slot + core)) * width
                    out[:, core * width : (core + 1) * width] = w_ref[:, at : at + width]


def run_stages(stages, blocks):
    held = [{} for _ in stages]
    for step in range(len(blocks) + 2 * len(stages)):
        for index, stage in enumerate(stages):
            at = step - 2 * index
            if 0 <= at < len(blocks):
                given = held[index - 1].pop(at) if index else ()
                held[index][at] = stage(blocks[at], *given)


def token_queries(q):
    lo, zero = low_lanes(q.shape[0]), jnp.zeros_like(q)
    return jnp.concatenate([jnp.where(lo, q, zero), jnp.where(lo, swap16(q), zero)], axis=0)


def inner_kernel(q_ref, k_ref, v_ref, x0, m0, lhs12, lhs3t, vk1, vk2, vk3, keys0, values0, scratch):
    heads, rows = q_ref.shape[0], q_ref.shape[1]
    blocks = rows // HALF
    lo = low_lanes(HALF)
    pairs, fours = group_matrix(HALF, 1), group_matrix(HALF, 2)

    def one_head(head, _):
        for block in range(blocks):
            at = slice(block * HALF, (block + 1) * HALF)
            put_pairs(keys0, values0, block, k_ref[head, at, :], v_ref[head, at, :])
        wide = jnp.concatenate([q_ref[head, block * HALF : (block + 1) * HALF, :] for block in range(blocks)], axis=1)
        wide2 = jnp.dot(pairs, wide, preferred_element_type=F32)
        wide3 = jnp.dot(fours, wide, preferred_element_type=F32)
        q_top = jnp.sum(q_ref[head].astype(F32), axis=0, keepdims=True)
        q_top = (q_top + swap(q_top)) * POOL ** (-0.5)

        def queries(block):
            at, lanes = slice(block * HALF, (block + 1) * HALF), slice(block * LANES, (block + 1) * LANES)
            q1, q2, q3 = (
                (sums + swap(sums)) * factor ** (-0.5)
                for sums, factor in ((q_ref[head, at, :].astype(F32), 2), (wide2[:, lanes], 4), (wide3[:, lanes], 8))
            )
            lhs12[head, at, :] = jnp.where(lo, q2, q1).astype(BF16)
            lhs3t[head, at, :] = jnp.where(lo, q_top, q3).astype(BF16)

        def scores(block):
            queries(block)
            if block in (0, blocks - 1):
                return (None,)
            q = q_ref[head, block * HALF : (block + 1) * HALF, :]
            return (scores_of(token_queries(q), keys0[(block - 1) * NR : (block + 2) * NR, :]),)

        def weights(block, s0):
            if s0 is None:
                return None, None
            m = jnp.max(s0, axis=1, keepdims=True)
            return m, jnp.exp2((s0 - m) * SCALE2).astype(BF16)

        def products(block, m, p0):
            if m is None:
                return
            at = slice((block - 1) * NR, block * NR)
            x0[head, at, :] = jnp.dot(p0, values0[(block - 1) * NR : (block + 2) * NR, :], preferred_element_type=F32)
            m0[head, at, :] = jnp.broadcast_to(m, (NR, LANES))

        run_stages((scores, weights, products), range(blocks))
        sums = fold_pairs(v_ref[head], k_ref[head])
        for level, out in enumerate((vk1, vk2, vk3), 1):
            if level > 1:
                sums = halve(scratch, sums)
            out[head] = pooled_vk(sums, 2**level)
        return 0

    lax.fori_loop(0, heads, one_head, 0)


def attend_kernel(
    head, q_ref, k_ref, v_ref, x0_in, m0_in, lhs12, lhs3t, vk1, vk2, vk3, first_in, second_in, tops, place,
    att, keys0, values0, halo_vk, scratch,
):
    own, rows = (vk1, vk2, vk3), q_ref.shape[1]
    blocks = rows // HALF
    even = lax.rem(place[0], 2) == 0
    for low in (True, False):

        def halo(index):
            at = slice(index * FAR, (index + 1) * FAR)
            sources = (second_in, first_in) if low else (first_in, second_in)
            return jnp.where(even, sources[0][head, at, :], sources[1][head, at, :])

        k, v = halo(0), halo(1)
        sums = fold_pairs(v, k)
        for level in range(1, LEVELS + 1):
            if level > 1:
                sums = halve(scratch, jnp.concatenate([beyond, sums] if low else [sums, beyond], axis=0))
            far = halo(level + 1)
            base = (2 * level - 2 + (not low)) * NR
            near_at, far_at = (base + FAR, base) if low else (base, base + FAR)
            halo_vk[near_at : near_at + HALF, :] = pooled_vk(sums, 2**level)
            halo_vk[far_at : far_at + FAR, :] = far
            beyond = far.astype(F32) * jnp.where(low_lanes(1), 2.0**level, 2.0 ** (level / 2))
        put_pairs(keys0, values0, 0 if low else 5, k, v)
        for index in range(2):
            start = index * HALF if low else rows - (2 - index) * HALF
            at = slice(start, start + HALF)
            put_pairs(keys0, values0, index + (1 if low else 3), k_ref[head, at, :], v_ref[head, at, :])

    def kept(level, half):
        mine = own[level - 1]
        count, at = mine.shape[1], (half // 2) * NR - NR
        spans = [(at, HALF), (at + 2 * NR, NR)] if half % 2 == 0 else [(at, NR), (at + 2 * NR + HALF, HALF)]
        pieces = []
        for start, size in spans:
            if 0 <= start < count:
                pieces.append(mine[head, start : start + size, :])
            else:
                start += (2 * level - 1) * NR - (count if start > 0 else 0)
                pieces.append(halo_vk[start : start + size, :])
        return jnp.concatenate(pieces, axis=0)

    def side_by_side(upper, lower):
        left = jnp.concatenate([upper, jnp.zeros((upper.shape[0], LANES), BF16)], axis=1)
        right = jnp.concatenate([jnp.zeros((lower.shape[0], LANES), BF16), lower], axis=1)
        return jnp.concatenate([left, right], axis=0)

    top = tops[head]
    positions = top.shape[0]
    lane = lax.broadcasted_iota(jnp.int32, (HALF, LANES), 1)
    distance = lane - HEAD_DIM - place[0]
    distance = jnp.where(distance < 0, distance + positions, distance)
    keep = (lane < HEAD_DIM) | ((distance >= 2) & (distance <= positions - 2))
    lo = low_lanes(HALF)

    def edge_window(block):
        return slice(0, 3 * NR) if block == 0 else slice(3 * NR, 6 * NR)

    def apart(x):
        low, zero = low_lanes(x.shape[0]), jnp.zeros_like(x)
        return jnp.concatenate([jnp.where(low, zero, x), jnp.where(low, zero, swap16(x))], axis=1)

    shared, shared_x, waiting, unfinished = {}, {}, [], []

    def scores(block):
        at = slice(block * HALF, (block + 1) * HALF)
        s12 = scores_of(apart(lhs12[head, at, :]), side_by_side(kept(1, block), kept(2, block // 2)))
        if block % 4 == 0:
            four = slice(block * HALF, (block + 4) * HALF)
            shared[block // 4] = scores_of(apart(lhs3t[head, four, :]), side_by_side(kept(3, block // 4), top))
        s3t = shared[block // 4][(block % 4) * HALF : (block % 4 + 1) * HALF]
        s0 = None
        if block in (0, blocks - 1):
            s0 = scores_of(token_queries(q_ref[head, at, :]), keys0[edge_window(block), :])
        return s0, s12, s3t

    def weights(block, s0, s12, s3t):
        masked = jnp.where(keep, s3t[:, LANES:], -jnp.inf)
        su = jnp.concatenate([s12, s3t[:, :LANES], masked], axis=1)
        mu = jnp.max(su, axis=1, keepdims=True)
        pu = jnp.exp2((su - mu) * SCALE2).astype(BF16)
        mu = jnp.concatenate([mu, mu], axis=0)
        if s0 is None:
            m0 = m0_in[head, (block - 1) * NR : block * NR, :]
            m = jnp.maximum(m0, mu)
            return None, jnp.exp2((m0 - m) * SCALE2), pu, jnp.exp2((mu - m) * SCALE2)
        m = jnp.maximum(jnp.max(s0, axis=1, keepdims=True), mu)
        return jnp.exp2((s0 - m) * SCALE2).astype(BF16), None, pu, jnp.exp2((mu - m) * SCALE2)

    def products(block, p0, share0, pu, share):
        values = ones_high(jnp.concatenate([kept(1, block), kept(2, block // 2)], axis=0))
        split = values.shape[0]
        xu = jnp.dot(pu[:, :split], values, preferred_element_type=F32)
        waiting.append(pu[:, split:])
        if block % 4 == 3:
            values = ones_high(jnp.concatenate([kept(3, block // 4), top], axis=0))
            shared_x[block // 4] = jnp.dot(jnp.concatenate(waiting, axis=0), values, preferred_element_type=F32)
            waiting.clear()
        if p0 is None:
            x = x0_in[head, (block - 1) * NR : block * NR, :] * share0
        else:
            x = jnp.dot(p0, values0[edge_window(block), :], preferred_element_type=F32)
        return x, xu, share

    def finish(block, x, xu, share):
        unfinished.append((block, x, xu, share))
        if block % 4 == 3:
            for item in unfinished:
                finish_one(*item)
            unfinished.clear()

    def finish_one(block, x, xu, share):
        xu = xu + shared_x[block // 4][(block % 4) * HALF : (block % 4 + 1) * HALF]
        x = x + jnp.concatenate([xu, xu], axis=0) * share
        x = x / swap(x)
        out = jnp.where(lo, x[:HALF], swap(x[HALF:]))
        att[0, block * HALF : (block + 1) * HALF, :] = out.astype(BF16)

    run_stages((scores, weights, products, finish), range(blocks))


def pair_weights(source, head, group):
    piece = source[head * HEAD_DIM : (head + 1) * HEAD_DIM, group * HEAD_DIM : (group + 1) * HEAD_DIM]
    zero = jnp.zeros_like(piece)
    return jnp.concatenate(
        [jnp.concatenate([piece, zero], axis=1), jnp.concatenate([zero, piece], axis=1)], axis=0
    )


def project_kernel(terms, *refs):
    count = len(terms)
    att, w, rest = refs[:count], refs[count : count + 2], refs[count + 2 :]
    earlier, outs = (rest[:2], rest[2:]) if len(rest) > 2 else (None, rest)
    heads = outs[0].shape[0]
    rows = jnp.concatenate([ref[...] for ref in att], axis=1)
    for core, out in enumerate(outs):
        for group in range(heads):
            columns = [pair_weights(w[source][...], head, core * heads + group) for source, head in terms]
            total = jnp.dot(rows, jnp.concatenate(columns, axis=0), preferred_element_type=F32)
            if earlier:
                total = total + earlier[core][group]
            out[group] = total.astype(out.dtype)


def add_kernel(mine, other, out, total, written):
    copies = []
    for head in range(total.shape[0]):
        total[head] = (mine[head] + other[head].astype(F32)).astype(BF16)
        copies.append(pltpu.make_async_copy(total.at[head], out.at[head], written.at[head]))
        copies[-1].start()
    for copy in copies:
        copy.wait()


def ring(count, step):
    return [(i, (i + step) % count) for i in range(count)]


def exchange(x, axis, bit):
    return lax.ppermute(x, axis, [(i, i ^ bit) for i in range(lax.axis_size(axis))])


def on_device(queries, keys, values, w_out):
    q, k, v = (jnp.transpose(x, (1, 0, 2)) for x in (queries, keys, values))
    heads, rows, _ = q.shape
    groups, count = lax.axis_size("head"), lax.axis_size("seq")
    params = pltpu.CompilerParams(vmem_limit_bytes=VMEM)
    vmem = pl.BlockSpec(memory_space=pltpu.VMEM)

    def shape(size, dtype=BF16):
        return jax.ShapeDtypeStruct((heads, size, LANES), dtype)

    place = lax.axis_index("seq").astype(jnp.int32).reshape(1)
    smem = pl.BlockSpec(memory_space=pltpu.SMEM)
    top, first_out, second_out = pl.pallas_call(
        prepare_kernel,
        in_specs=[pl.BlockSpec(memory_space=pltpu.HBM)] * 2 + [smem],
        out_specs=[vmem] * 3,
        out_shape=[jax.ShapeDtypeStruct((count, heads, LANES), BF16)] + [shape(HALO_ROWS)] * 2,
        scratch_shapes=[pltpu.VMEM((heads, rows, LANES), BF16)] * 2
        + [pltpu.VMEM((heads, rows, LANES), F32), pltpu.SemaphoreType.DMA((heads, 2))],
        compiler_params=pltpu.CompilerParams(vmem_limit_bytes=60 * 1024 * 1024),
        name="prepare",
    )(k, v, place)
    first_in = exchange(first_out, "seq", 1)
    second_in = lax.ppermute(second_out, "seq", [(i, (i - 1 if i % 2 == 0 else i + 1) % count) for i in range(count)])
    tops = lax.all_to_all(top, "seq", split_axis=0, concat_axis=0, tiled=True).transpose(1, 0, 2)
    top, w_out = lax.optimization_barrier((top, w_out))
    width = w_out.shape[1] // groups
    me = jnp.full((1, groups), lax.axis_index("head"), jnp.int32)
    w_own, w_far = pl.pallas_call(
        cut_kernel,
        in_specs=[vmem, pl.BlockSpec(memory_space=pltpu.SMEM)],
        out_shape=[jax.ShapeDtypeStruct((w_out.shape[0], 2 * width), BF16)] * 2,
        compiler_params=params,
        name="cut",
    )(w_out, me)
    w_far = exchange(w_far, "head", 2)

    tops, first_in, q = lax.optimization_barrier((tops, first_in, q))
    pooled = [rows >> level for level in range(LEVELS)]
    inner = pl.pallas_call(
        inner_kernel,
        in_specs=[vmem] * 3,
        out_specs=[vmem] * 7,
        out_shape=[shape(2 * rows - 2 * NR, F32)] * 2 + [shape(rows)] * 2 + [shape(size) for size in pooled],
        scratch_shapes=[pltpu.VMEM((2 * rows, LANES), BF16)] * 2 + [pltpu.VMEM((rows, LANES), F32)],
        compiler_params=params,
        cost_estimate=pl.CostEstimate(flops=4_000_000_000, bytes_accessed=8_000_000, transcendentals=1_000_000),
        name="inner",
    )(q, k, v)
    parts = {}
    for head in range(heads):
        att = pl.pallas_call(
            functools.partial(attend_kernel, head),
            in_specs=[vmem] * 13 + [smem],
            out_shape=jax.ShapeDtypeStruct((1, rows, LANES), BF16),
            scratch_shapes=[pltpu.VMEM((6 * NR, LANES), BF16)] * 3 + [pltpu.VMEM((NR, LANES), F32)],
            compiler_params=params,
            name=f"attend{head}",
        )(q, k, v, *inner, first_in, second_in, tops, place)[0]
        parts[0, head], parts[1, head] = att, exchange(att, "head", 2)
    late = [(1, LAST)]
    early = [term for term in parts if term not in late]
    shares = []
    for terms, types in ((early, (F32, F32)), (late, (F32, BF16))):
        shares = pl.pallas_call(
            functools.partial(project_kernel, terms),
            in_specs=[vmem] * (len(terms) + 2 + len(shares)),
            out_specs=[vmem] * 2,
            out_shape=[shape(rows, dtype) for dtype in types],
            compiler_params=params,
            name="project",
        )(*[parts[term] for term in terms], w_own, w_far, *shares)
    out = pl.pallas_call(
        add_kernel,
        in_specs=[vmem] * 2,
        out_specs=pl.BlockSpec(memory_space=pltpu.HBM),
        scratch_shapes=[pltpu.VMEM((heads, rows, LANES), BF16), pltpu.SemaphoreType.DMA((heads,))],
        out_shape=shape(rows),
        compiler_params=params,
        name="add",
    )(shares[0], exchange(shares[1], "head", 1))
    return jnp.transpose(out, (1, 0, 2))


def solution(mesh):
    return jax.shard_map(
        on_device,
        mesh=mesh,
        in_specs=(
            P("seq", "head", None),
            P("seq", "head", None),
            P("seq", "head", None),
            P("head", None),
        ),
        out_specs=P("seq", "head", None),
        check_vma=False,
    )
```

profile of v0, /device:TPU:1, one launch (start us, length us, event | category | flops | bytes accessed | tf_op | source)
XLA Modules:
  0.0 49.2 jit_solution(11721948007300398747)
XLA Ops:
  0.0 0.0 copy-start.1
  0.0 0.0 copy-start
  0.0 0.0 copy-start.2
  0.0 2.6 %prepare.1 = (bf16[64,3,128]{2,1,0:T(4,128)(2,1)}, bf16[3,320,128]{2,1,0:T(8,128)(2,1)}, bf16[3,320,128]{2,1,0:T(8,128)(2,1)}) custom-call(bf16[3,512,128]{2,1,0:T(8,128)(2,1)} %bitcast.11, bf16[3,512,128]{2,1,0:T(8,128)(2,1)} %bitcast.16, s32[1]{0:T(128)} %bitcast.2.place), custom_call_target="tpu_custom_call" | custom-call | tf_op jit(solution)/shard_map/prepare/pallas_call | solution.py:368
  2.6 3.7 %collective-permute-start = (bf16[3,320,128]{2,1,0:T(8,128)(2,1)}, bf16[3,320,128]{2,1,0:T(8,128)(2,1)S(1)}, u32[]{:S(2)}, u32[]{:S(2)}) collective-permute-start(bf16[3,320,128]{2,1,0:T(8,128)(2,1)} %get-tuple-element.26), channel_id=1, source_target_pairs={{0,4},{4,0},{8,12},{12,8},{16,20},{20,16},{24,28},{28,24},{32,36},... | collective-permute-start | bytes 737288 | tf_op jit(solution)/shard_map/ppermute | solution.py:353
  6.3 11.8 %all-to-all-start = ((bf16[64,3,128]{2,1,0:T(4,128)(2,1)}), bf16[64,3,128]{2,1,0:T(4,128)(2,1)S(1)}, u32[]{:S(2)}, u32[]{:S(2)}) async-start(bf16[64,3,128]{2,1,0:T(4,128)(2,1)} %get-tuple-element.25), calls=%async_computation | async-start | bytes 131072 | tf_op jit(solution)/shard_map/all_to_all | solution.py:380
  18.1 7.1 %collective-permute-start.1 = (bf16[3,320,128]{2,1,0:T(8,128)(2,1)}, bf16[3,320,128]{2,1,0:T(8,128)(2,1)S(1)}, u32[]{:S(2)}, u32[]{:S(2)}) collective-permute-start(bf16[3,320,128]{2,1,0:T(8,128)(2,1)} %get-tuple-element.36), channel_id=1, source_target_pairs={{0,252},{4,8},{8,4},{12,16},{16,12},{20,24},{24,20},{28,32},{32,28... | collective-permute-start | bytes 737288 | tf_op jit(solution)/shard_map/ppermute | solution.py:379
  25.2 1.0 %copy-done.3 = bf16[192,768]{1,0:T(8,128)(2,1)S(1)} copy-done((bf16[192,768]{1,0:T(8,128)(2,1)S(1)}, bf16[192,768]{1,0:T(8,128)(2,1)}, u32[]{:S(2)}) %copy-start.3) | copy-done | bytes 294936
  26.2 0.7 %cut.1 = (bf16[192,384]{1,0:T(8,128)(2,1)S(1)}, bf16[192,384]{1,0:T(8,128)(2,1)S(1)}) custom-call(bf16[192,768]{1,0:T(8,128)(2,1)S(1)} %copy-done.3, s32[1,4]{1,0:T(1,128)S(1)} %broadcast_in_dim.3.me), custom_call_target="tpu_custom_call" | custom-call | tf_op jit(solution)/shard_map/cut/pallas_call | solution.py:384
  26.9 1.2 %collective-permute-start.3 = (bf16[192,384]{1,0:T(8,128)(2,1)S(1)}, bf16[192,384]{1,0:T(8,128)(2,1)S(1)}, u32[]{:S(2)}, u32[]{:S(2)}) collective-permute-start(bf16[192,384]{1,0:T(8,128)(2,1)S(1)} %get-tuple-element.40), channel_id=1, source_target_pairs={{0,2},{1,3},{2,0},{3,1},{4,6},{5,7},{6,4},{7,5},{8,10},{9,11},{10,... | collective-permute-start | bytes 442376 | tf_op jit(solution)/shard_map/ppermute | solution.py:353
  28.2 1.0 %all-to-all-done = bf16[64,3,128]{2,1,0:T(4,128)(2,1)S(1)} async-done(((bf16[64,3,128]{2,1,0:T(4,128)(2,1)}), bf16[64,3,128]{2,1,0:T(4,128)(2,1)S(1)}, u32[]{:S(2)}, u32[]{:S(2)}) %all-to-all-start) | async-done | bytes 49184 | tf_op jit(solution)/shard_map/all_to_all | solution.py:380
  29.2 0.0 collective-permute-done.first_in
  29.2 0.0 copy-done.1
  29.2 0.0 copy-done
  29.2 0.0 copy-done.2
  29.2 2.9 %inner.1 = (f32[3,768,128]{2,1,0:T(8,128)S(1)}, f32[3,768,128]{2,1,0:T(8,128)S(1)}, bf16[3,512,128]{2,1,0:T(8,128)(2,1)S(1)}, bf16[3,512,128]{2,1,0:T(8,128)(2,1...) custom-call(bf16[3,512,128]{2,1,0:T(8,128)(2,1)S(1)} %bitcast.21, ...), custom_call_target="tpu_custom_call" | custom-call | flops 4000000000 | bytes 8000000 | tf_op jit(solution)/shard_map/inner/pallas_call | solution.py:395
  32.1 0.0 collective-permute-done.1.second_in
  32.1 1.5 %attend0.1 = bf16[1,512,128]{2,1,0:T(8,128)(2,1)S(1)} custom-call(bf16[3,512,128]{2,1,0:T(8,128)(2,1)S(1)} %bitcast.22, bf16[3,512,128]{2,1,0:T(8,128)(2,1)S(1)} %bitcast.13, bf16[3,512,128]{2,1,0:T(8,128)(2,1)S(1)} %bitcast.18, f32[3,768,128]{2,1,0:T(8,128)S(1)} %get-tuple-element.28.x0_in, f32[3,768,128]{2,1,0:T(8,128)S(1)} %get-tuple-element.29.m0_in, ...), custom_call_target="tpu_custom_call" | custom-call | tf_op jit(solution)/shard_map/attend0/pallas_call | solution.py:407
  33.6 1.2 %collective-permute-start.4 = (bf16[512,128]{1,0:T(8,128)(2,1)S(1)}, bf16[512,128]{1,0:T(8,128)(2,1)S(1)}, u32[]{:S(2)}, u32[]{:S(2)}) collective-permute-start(bf16[512,128]{1,0:T(8,128)(2,1)S(1)} %bitcast.28), channel_id=1, source_target_pairs={{0,2},{1,3},{2,0},{3,1},{4,6},{5,7},{6,4},{7,5},{8,10},{9,11},{10,... | collective-permute-start | bytes 393224 | tf_op jit(solution)/shard_map/ppermute | solution.py:353
  34.9 1.5 %attend1.1 = bf16[1,512,128]{2,1,0:T(8,128)(2,1)S(1)} custom-call(bf16[3,512,128]{2,1,0:T(8,128)(2,1)S(1)} %bitcast.23, bf16[3,512,128]{2,1,0:T(8,128)(2,1)S(1)} %bitcast.14, bf16[3,512,128]{2,1,0:T(8,128)(2,1)S(1)} %bitcast.19, f32[3,768,128]{2,1,0:T(8,128)S(1)} %get-tuple-element.28.x0_in, f32[3,768,128]{2,1,0:T(8,128)S(1)} %get-tuple-element.29.m0_in, ...), custom_call_target="tpu_custom_call" | custom-call | tf_op jit(solution)/shard_map/attend1/pallas_call | solution.py:407
  36.3 0.4 collective-permute-start.5
  36.7 1.5 %attend2.1 = bf16[1,512,128]{2,1,0:T(8,128)(2,1)S(1)} custom-call(bf16[3,512,128]{2,1,0:T(8,128)(2,1)S(1)} %bitcast.24, bf16[3,512,128]{2,1,0:T(8,128)(2,1)S(1)} %bitcast.15, bf16[3,512,128]{2,1,0:T(8,128)(2,1)S(1)} %bitcast.20, f32[3,768,128]{2,1,0:T(8,128)S(1)} %get-tuple-element.28.x0_in, f32[3,768,128]{2,1,0:T(8,128)S(1)} %get-tuple-element.29.m0_in, ...), custom_call_target="tpu_custom_call" | custom-call | tf_op jit(solution)/shard_map/attend2/pallas_call | solution.py:407
  38.2 1.2 %collective-permute-start.2 = (bf16[512,128]{1,0:T(8,128)(2,1)S(1)}, bf16[512,128]{1,0:T(8,128)(2,1)S(1)}, u32[]{:S(2)}, u32[]{:S(2)}) collective-permute-start(bf16[512,128]{1,0:T(8,128)(2,1)S(1)} %bitcast.32), channel_id=1, source_target_pairs={{0,2},{1,3},{2,0},{3,1},{4,6},{5,7},{6,4},{7,5},{8,10},{9,11},{10,... | collective-permute-start | bytes 393224 | tf_op jit(solution)/shard_map/ppermute | solution.py:353
  39.4 0.0 collective-permute-done.3.refs_6_.refs_2_
  39.4 0.0 collective-permute-done.4.refs_1_
  39.4 2.3 %collective-permute-done.5.refs_3_ = bf16[512,128]{1,0:T(8,128)(2,1)S(1)} collective-permute-done((bf16[512,128]{1,0:T(8,128)(2,1)S(1)}, bf16[512,128]{1,0:T(8,128)(2,1)S(1)}, u32[]{:S(2)}, u32[]{:S(2)}) %collective-permute-start.5) | collective-permute-done | bytes 131104 | tf_op jit(solution)/shard_map/ppermute | solution.py:353
  41.8 1.2 %project.2 = (f32[3,512,128]{2,1,0:T(8,128)S(1)}, f32[3,512,128]{2,1,0:T(8,128)S(1)}) custom-call(bf16[512,128]{1,0:T(8,128)(2,1)S(1)} %bitcast.29, bf16[512,128]{1,0:T(8,128)(2,1)S(1)} %collective-permute-done.4.refs_1_, bf16[512,128]{1,0:T(8,128)(2,1)S(1)} %bitcast.31, bf16[512,128]{1,0:T(8,128)(2,1)S(1)} %collective-permute-done.5.refs_3_, ...), custom_call_target="tpu_custom_call" | custom-call | tf_op jit(solution)/shard_map/project/pallas_call | solution.py:420
  43.0 1.3 %collective-permute-done.2.refs_0_ = bf16[512,128]{1,0:T(8,128)(2,1)S(1)} collective-permute-done((bf16[512,128]{1,0:T(8,128)(2,1)S(1)}, bf16[512,128]{1,0:T(8,128)(2,1)S(1)}, u32[]{:S(2)}, u32[]{:S(2)}) %collective-permute-start.2) | collective-permute-done | bytes 131104 | tf_op jit(solution)/shard_map/ppermute | solution.py:353
  44.3 0.4 project.3
  44.7 2.3 %collective-permute-start.6 = (bf16[3,512,128]{2,1,0:T(8,128)(2,1)S(1)}, bf16[3,512,128]{2,1,0:T(8,128)(2,1)S(1)}, u32[]{:S(2)}, u32[]{:S(2)}) collective-permute-start(bf16[3,512,128]{2,1,0:T(8,128)(2,1)S(1)} %get-tuple-element.44), channel_id=1, source_target_pairs={{0,1},{1,0},{2,3},{3,2},{4,5},{5,4},{6,7},{7,6},{8,9},{9,8},{10,11... | collective-permute-start | bytes 1179656 | tf_op jit(solution)/shard_map/ppermute | solution.py:353
  47.1 1.3 %collective-permute-done.6.other = bf16[3,512,128]{2,1,0:T(8,128)(2,1)S(1)} collective-permute-done((bf16[3,512,128]{2,1,0:T(8,128)(2,1)S(1)}, bf16[3,512,128]{2,1,0:T(8,128)(2,1)S(1)}, u32[]{:S(2)}, u32[]{:S(2)}) %collective-permute-start.6) | collective-permute-done | bytes 393248 | tf_op jit(solution)/shard_map/ppermute | solution.py:353
  48.4 0.8 %add.1 = bf16[3,512,128]{2,1,0:T(8,128)(2,1)} custom-call(f32[3,512,128]{2,1,0:T(8,128)S(1)} %get-tuple-element.43.mine, bf16[3,512,128]{2,1,0:T(8,128)(2,1)S(1)} %collective-permute-done.6.other), custom_call_target="tpu_custom_call" | custom-call | tf_op jit(solution)/shard_map/add/pallas_call | solution.py:428
  (3 shorter events, 0.0 us)
Async XLA Ops:
  0.0 29.2 %copy-start.1 = (bf16[512,3,128]{2,0,1:T(8,128)(2,1)S(1)}, bf16[512,3,128]{2,0,1:T(8,128)(2,1)}, u32[]{:S(2)}) copy-start(bf16[512,3,128]{2,0,1:T(8,128)(2,1)} %param.6) | copy-start | bytes 1179652
  0.0 29.2 %copy-start = (bf16[512,3,128]{2,0,1:T(8,128)(2,1)S(1)}, bf16[512,3,128]{2,0,1:T(8,128)(2,1)}, u32[]{:S(2)}) copy-start(bf16[512,3,128]{2,0,1:T(8,128)(2,1)} %param.5) | copy-start | bytes 1179652
  0.0 29.2 %copy-start.2 = (bf16[512,3,128]{2,0,1:T(8,128)(2,1)S(1)}, bf16[512,3,128]{2,0,1:T(8,128)(2,1)}, u32[]{:S(2)}) copy-start(bf16[512,3,128]{2,0,1:T(8,128)(2,1)} %param.4) | copy-start | bytes 1179652
  2.6 26.6 %collective-permute-start = (bf16[3,320,128]{2,1,0:T(8,128)(2,1)}, bf16[3,320,128]{2,1,0:T(8,128)(2,1)S(1)}, u32[]{:S(2)}, u32[]{:S(2)}) collective-permute-start(bf16[3,320,128]{2,1,0:T(8,128)(2,1)} %get-tuple-element.26), channel_id=1, source_target_pairs={{0,4},{4,0},{8,12},{12,8},{16,20},{20,16},{24,28},{28,24},{32,36},... | collective-permute-start | bytes 737288 | tf_op jit(solution)/shard_map/ppermute | solution.py:353
  6.3 22.9 %all-to-all-start = ((bf16[64,3,128]{2,1,0:T(4,128)(2,1)}), bf16[64,3,128]{2,1,0:T(4,128)(2,1)S(1)}, u32[]{:S(2)}, u32[]{:S(2)}) async-start(bf16[64,3,128]{2,1,0:T(4,128)(2,1)} %get-tuple-element.25), calls=%async_computation | async-start | bytes 131072 | tf_op jit(solution)/shard_map/all_to_all | solution.py:380
  18.1 14.0 %collective-permute-start.1 = (bf16[3,320,128]{2,1,0:T(8,128)(2,1)}, bf16[3,320,128]{2,1,0:T(8,128)(2,1)S(1)}, u32[]{:S(2)}, u32[]{:S(2)}) collective-permute-start(bf16[3,320,128]{2,1,0:T(8,128)(2,1)} %get-tuple-element.36), channel_id=1, source_target_pairs={{0,252},{4,8},{8,4},{12,16},{16,12},{20,24},{24,20},{28,32},{32,28... | collective-permute-start | bytes 737288 | tf_op jit(solution)/shard_map/ppermute | solution.py:379
  25.2 1.0 %copy-start.3 = (bf16[192,768]{1,0:T(8,128)(2,1)S(1)}, bf16[192,768]{1,0:T(8,128)(2,1)}, u32[]{:S(2)}) copy-start(bf16[192,768]{1,0:T(8,128)(2,1)} %w_ref) | copy-start | bytes 884740
  26.9 12.5 %collective-permute-start.3 = (bf16[192,384]{1,0:T(8,128)(2,1)S(1)}, bf16[192,384]{1,0:T(8,128)(2,1)S(1)}, u32[]{:S(2)}, u32[]{:S(2)}) collective-permute-start(bf16[192,384]{1,0:T(8,128)(2,1)S(1)} %get-tuple-element.40), channel_id=1, source_target_pairs={{0,2},{1,3},{2,0},{3,1},{4,6},{5,7},{6,4},{7,5},{8,10},{9,11},{10,... | collective-permute-start | bytes 442376 | tf_op jit(solution)/shard_map/ppermute | solution.py:353
  33.6 5.8 %collective-permute-start.4 = (bf16[512,128]{1,0:T(8,128)(2,1)S(1)}, bf16[512,128]{1,0:T(8,128)(2,1)S(1)}, u32[]{:S(2)}, u32[]{:S(2)}) collective-permute-start(bf16[512,128]{1,0:T(8,128)(2,1)S(1)} %bitcast.28), channel_id=1, source_target_pairs={{0,2},{1,3},{2,0},{3,1},{4,6},{5,7},{6,4},{7,5},{8,10},{9,11},{10,... | collective-permute-start | bytes 393224 | tf_op jit(solution)/shard_map/ppermute | solution.py:353
  36.3 5.4 %collective-permute-start.5 = (bf16[512,128]{1,0:T(8,128)(2,1)S(1)}, bf16[512,128]{1,0:T(8,128)(2,1)S(1)}, u32[]{:S(2)}, u32[]{:S(2)}) collective-permute-start(bf16[512,128]{1,0:T(8,128)(2,1)S(1)} %bitcast.30), channel_id=1, source_target_pairs={{0,2},{1,3},{2,0},{3,1},{4,6},{5,7},{6,4},{7,5},{8,10},{9,11},{10,... | collective-permute-start | bytes 393224 | tf_op jit(solution)/shard_map/ppermute | solution.py:353
  38.2 6.1 %collective-permute-start.2 = (bf16[512,128]{1,0:T(8,128)(2,1)S(1)}, bf16[512,128]{1,0:T(8,128)(2,1)S(1)}, u32[]{:S(2)}, u32[]{:S(2)}) collective-permute-start(bf16[512,128]{1,0:T(8,128)(2,1)S(1)} %bitcast.32), channel_id=1, source_target_pairs={{0,2},{1,3},{2,0},{3,1},{4,6},{5,7},{6,4},{7,5},{8,10},{9,11},{10,... | collective-permute-start | bytes 393224 | tf_op jit(solution)/shard_map/ppermute | solution.py:353
  44.7 3.7 %collective-permute-start.6 = (bf16[3,512,128]{2,1,0:T(8,128)(2,1)S(1)}, bf16[3,512,128]{2,1,0:T(8,128)(2,1)S(1)}, u32[]{:S(2)}, u32[]{:S(2)}) collective-permute-start(bf16[3,512,128]{2,1,0:T(8,128)(2,1)S(1)} %get-tuple-element.44), channel_id=1, source_target_pairs={{0,1},{1,0},{2,3},{3,2},{4,5},{5,4},{6,7},{7,6},{8,9},{9,8},{10,11... | collective-permute-start | bytes 1179656 | tf_op jit(solution)/shard_map/ppermute | solution.py:353
where the time goes:
time: 49.4 us; the launch traced here: 49.2 us
  starting transfers between devices  29.1 us (59%)
  Pallas kernels  13.1 us (27%)
  waiting for transfers between devices  5.97 us (12%)
  local copies, waits for them, and re-layouts  0.98 us (2%)
    all_to_all x1, starting transfers between devices, on_device(): lax.all_to_all(top, 'seq', split_axis=0, concat_axis=0, tiled=True)  11.8 us
    ppermute x6, starting transfers between devices, exchange(): lax.ppermute(x, axis, [(i, i ^ bit) for i in range(lax.axis_size(axis))])  10.1 us
    ppermute x1, starting transfers between devices, on_device(): lax.ppermute(second_out, 'seq', [(i, (i - 1 if i % 2 == 0 else i + 1) % c...  7.13 us
    ppermute x6, waiting for transfers between devices, exchange(): lax.ppermute(x, axis, [(i, i ^ bit) for i in range(lax.axis_size(axis))])  4.98 us
    pallas_call x3, Pallas kernels, on_device(): pl.pallas_call(functools.partial(attend_kernel, head), in_specs=[vmem] *...  4.4 us
    pallas_call x1, Pallas kernels, on_device(): pl.pallas_call(inner_kernel, in_specs=[vmem] * 3, out_specs=[vmem] * 7, o...  2.91 us
    pallas_call x1, Pallas kernels, on_device(): pl.pallas_call(prepare_kernel, in_specs=[pl.BlockSpec(memory_space=pltpu....  2.57 us
    pallas_call x2, Pallas kernels, on_device(): pl.pallas_call(functools.partial(project_kernel, terms), in_specs=[vmem]...  1.65 us
  transfers between devices with their start and end apart: 8, of which 4 were waited for; matrix products, arithmetic and copies ran while one was open for 0% of the time, Pallas kernels for 19%

commit v1 on v0

--- a/solution.py
+++ b/solution.py
@@ -85,6 +85,7 @@
     for pair in loads:
         for copy in pair:
             copy.start()
+    coarse = []
     for head in range(heads):
         for copy in loads[head]:
             copy.wait()
@@ -103,7 +104,10 @@
             at = slice(index * FAR, (index + 1) * FAR)
             first_out[head, at, :] = jnp.where(even, high, low)
             second_out[head, at, :] = jnp.where(even, low, high)
-        top[:, head, :] = jnp.broadcast_to(pooled_vk(jnp.sum(sums, axis=0, keepdims=True), POOL), (top.shape[0], LANES))
+        coarse.append(jnp.sum(sums, axis=0, keepdims=True))
+    rows = pooled_vk(jnp.concatenate(coarse, axis=0), POOL)
+    for position in range(top.shape[0]):
+        top[position] = rows
 
 
 def cut_kernel(w_ref, me, *outs):
@@ -139,54 +143,56 @@
     lo = low_lanes(HALF)
     pairs, fours = group_matrix(HALF, 1), group_matrix(HALF, 2)
 
-    def one_head(head, _):
-        for block in range(blocks):
-            at = slice(block * HALF, (block + 1) * HALF)
-            put_pairs(keys0, values0, block, k_ref[head, at, :], v_ref[head, at, :])
-        wide = jnp.concatenate([q_ref[head, block * HALF : (block + 1) * HALF, :] for block in range(blocks)], axis=1)
-        wide2 = jnp.dot(pairs, wide, preferred_element_type=F32)
-        wide3 = jnp.dot(fours, wide, preferred_element_type=F32)
-        q_top = jnp.sum(q_ref[head].astype(F32), axis=0, keepdims=True)
-        q_top = (q_top + swap(q_top)) * POOL ** (-0.5)
-
-        def queries(block):
-            at, lanes = slice(block * HALF, (block + 1) * HALF), slice(block * LANES, (block + 1) * LANES)
-            q1, q2, q3 = (
-                (sums + swap(sums)) * factor ** (-0.5)
-                for sums, factor in ((q_ref[head, at, :].astype(F32), 2), (wide2[:, lanes], 4), (wide3[:, lanes], 8))
-            )
-            lhs12[head, at, :] = jnp.where(lo, q2, q1).astype(BF16)
-            lhs3t[head, at, :] = jnp.where(lo, q_top, q3).astype(BF16)
-
-        def scores(block):
-            queries(block)
-            if block in (0, blocks - 1):
-                return (None,)
-            q = q_ref[head, block * HALF : (block + 1) * HALF, :]
-            return (scores_of(token_queries(q), keys0[(block - 1) * NR : (block + 2) * NR, :]),)
-
-        def weights(block, s0):
-            if s0 is None:
-                return None, None
-            m = jnp.max(s0, axis=1, keepdims=True)
-            return m, jnp.exp2((s0 - m) * SCALE2).astype(BF16)
-
-        def products(block, m, p0):
-            if m is None:
-                return
-            at = slice((block - 1) * NR, block * NR)
-            x0[head, at, :] = jnp.dot(p0, values0[(block - 1) * NR : (block + 2) * NR, :], preferred_element_type=F32)
-            m0[head, at, :] = jnp.broadcast_to(m, (NR, LANES))
-
-        run_stages((scores, weights, products), range(blocks))
-        sums = fold_pairs(v_ref[head], k_ref[head])
-        for level, out in enumerate((vk1, vk2, vk3), 1):
-            if level > 1:
-                sums = halve(scratch, sums)
-            out[head] = pooled_vk(sums, 2**level)
-        return 0
-
-    lax.fori_loop(0, heads, one_head, 0)
+    shared = {}
+
+    def start(task):
+        head, block = task
+        if block == 0:
+            for index in range(blocks):
+                at = slice(index * HALF, (index + 1) * HALF)
+                put_pairs(keys0.at[head], values0.at[head], index, k_ref[head, at, :], v_ref[head, at, :])
+            wide = jnp.concatenate([q_ref[head, i * HALF : (i + 1) * HALF, :] for i in range(blocks)], axis=1)
+            wide2 = jnp.dot(pairs, wide, preferred_element_type=F32)
+            wide3 = jnp.dot(fours, wide, preferred_element_type=F32)
+            q_top = jnp.sum(q_ref[head].astype(F32), axis=0, keepdims=True)
+            shared[head] = wide2, wide3, (q_top + swap(q_top)) * POOL ** (-0.5)
+        if block == 4:
+            sums = fold_pairs(v_ref[head], k_ref[head])
+            for level, out in enumerate((vk1, vk2, vk3), 1):
+                if level > 1:
+                    sums = halve(scratch.at[head], sums)
+                out[head] = pooled_vk(sums, 2**level)
+        return ()
+
+    def scores(task):
+        head, block = task
+        at, lanes = slice(block * HALF, (block + 1) * HALF), slice(block * LANES, (block + 1) * LANES)
+        wide2, wide3, q_top = shared[head]
+        q1, q2, q3 = (
+            (sums + swap(sums)) * factor ** (-0.5)
+            for sums, factor in ((q_ref[head, at, :].astype(F32), 2), (wide2[:, lanes], 4), (wide3[:, lanes], 8))
+        )
+        lhs12[head, at, :] = jnp.where(lo, q2, q1).astype(BF16)
+        lhs3t[head, at, :] = jnp.where(lo, q_top, q3).astype(BF16)
+        if block in (0, blocks - 1):
+            return (None,)
+        return (scores_of(token_queries(q_ref[head, at, :]), keys0[head, (block - 1) * NR : (block + 2) * NR, :]),)
+
+    def weights(task, s0):
+        if s0 is None:
+            return None, None
+        m = jnp.max(s0, axis=1, keepdims=True)
+        return m, jnp.exp2((s0 - m) * SCALE2).astype(BF16)
+
+    def products(task, m, p0):
+        head, block = task
+        if m is None:
+            return
+        at, window = slice((block - 1) * NR, block * NR), slice((block - 1) * NR, (block + 2) * NR)
+        x0[head, at, :] = jnp.dot(p0, values0[head, window, :], preferred_element_type=F32)
+        m0[head, at, :] = jnp.broadcast_to(m, (NR, LANES))
+
+    run_stages((start, scores, weights, products), [(head, block) for head in range(heads) for block in range(blocks)])
 
 
 def attend_kernel(
@@ -397,7 +403,7 @@
         in_specs=[vmem] * 3,
         out_specs=[vmem] * 7,
         out_shape=[shape(2 * rows - 2 * NR, F32)] * 2 + [shape(rows)] * 2 + [shape(size) for size in pooled],
-        scratch_shapes=[pltpu.VMEM((2 * rows, LANES), BF16)] * 2 + [pltpu.VMEM((rows, LANES), F32)],
+        scratch_shapes=[pltpu.VMEM((heads, 2 * rows, LANES), BF16)] * 2 + [pltpu.VMEM((heads, rows, LANES), F32)],
         compiler_params=params,
         cost_estimate=pl.CostEstimate(flops=4_000_000_000, bytes_accessed=8_000_000, transcendentals=1_000_000),
         name="inner",

time: 49.4 us -> 49.3 us (level)
  transfers between devices with their start and end apart: 8 -> 8, of which waited for: 4 -> 5; matrix products, arithmetic and copies ran while one was open for 0% -> 0% of each run, Pallas kernels for 19% -> 18%
where the time goes in v1:
time: 49.3 us; the launch traced here: 49.1 us
  starting transfers between devices  28.9 us (59%)
  Pallas kernels  12.8 us (26%)
  waiting for transfers between devices  6.33 us (13%)
  local copies, waits for them, and re-layouts  0.98 us (2%)
    all_to_all x1, starting transfers between devices, on_device(): lax.all_to_all(top, 'seq', split_axis=0, concat_axis=0, tiled=True)  11.8 us
    ppermute x6, starting transfers between devices, exchange(): lax.ppermute(x, axis, [(i, i ^ bit) for i in range(lax.axis_size(axis))])  9.92 us
    ppermute x1, starting transfers between devices, on_device(): lax.ppermute(second_out, 'seq', [(i, (i - 1 if i % 2 == 0 else i + 1) % c...  7.13 us
    ppermute x6, waiting for transfers between devices, exchange(): lax.ppermute(x, axis, [(i, i ^ bit) for i in range(lax.axis_size(axis))])  5.13 us
    pallas_call x3, Pallas kernels, on_device(): pl.pallas_call(functools.partial(attend_kernel, head), in_specs=[vmem] *...  4.38 us
    pallas_call x1, Pallas kernels, on_device(): pl.pallas_call(inner_kernel, in_specs=[vmem] * 3, out_specs=[vmem] * 7, o...  2.69 us
    pallas_call x1, Pallas kernels, on_device(): pl.pallas_call(prepare_kernel, in_specs=[pl.BlockSpec(memory_space=pltpu....  2.54 us
    pallas_call x2, Pallas kernels, on_device(): pl.pallas_call(functools.partial(project_kernel, terms), in_specs=[vmem]...  1.66 us
  transfers between devices with their start and end apart: 8, of which 5 were waited for; matrix products, arithmetic and copies ran while one was open for 0% of the time, Pallas kernels for 18%

profile of v1, /device:TPU:1, one launch (start us, length us, event | category | flops | bytes accessed | tf_op | source)
XLA Modules:
  0.0 49.1 jit_solution(14308281085764093166)
XLA Ops:
  0.0 0.0 copy-start.1
  0.0 0.0 copy-start
  0.0 0.0 copy-start.2
  0.0 2.5 %prepare.1 = (bf16[64,3,128]{2,1,0:T(4,128)(2,1)}, bf16[3,320,128]{2,1,0:T(8,128)(2,1)}, bf16[3,320,128]{2,1,0:T(8,128)(2,1)}) custom-call(bf16[3,512,128]{2,1,0:T(8,128)(2,1)} %bitcast.11, bf16[3,512,128]{2,1,0:T(8,128)(2,1)} %bitcast.16, s32[1]{0:T(128)} %bitcast.2.place), custom_call_target="tpu_custom_call" | custom-call | tf_op jit(solution)/shard_map/prepare/pallas_call | solution.py:374
  2.6 3.7 %collective-permute-start = (bf16[3,320,128]{2,1,0:T(8,128)(2,1)}, bf16[3,320,128]{2,1,0:T(8,128)(2,1)S(1)}, u32[]{:S(2)}, u32[]{:S(2)}) collective-permute-start(bf16[3,320,128]{2,1,0:T(8,128)(2,1)} %get-tuple-element.26), channel_id=1, source_target_pairs={{0,4},{4,0},{8,12},{12,8},{16,20},{20,16},{24,28},{28,24},{32,36},... | collective-permute-start | bytes 737288 | tf_op jit(solution)/shard_map/ppermute | solution.py:359
  6.2 11.8 %all-to-all-start = ((bf16[64,3,128]{2,1,0:T(4,128)(2,1)}), bf16[64,3,128]{2,1,0:T(4,128)(2,1)S(1)}, u32[]{:S(2)}, u32[]{:S(2)}) async-start(bf16[64,3,128]{2,1,0:T(4,128)(2,1)} %get-tuple-element.25), calls=%async_computation | async-start | bytes 131072 | tf_op jit(solution)/shard_map/all_to_all | solution.py:386
  18.1 7.1 %collective-permute-start.1 = (bf16[3,320,128]{2,1,0:T(8,128)(2,1)}, bf16[3,320,128]{2,1,0:T(8,128)(2,1)S(1)}, u32[]{:S(2)}, u32[]{:S(2)}) collective-permute-start(bf16[3,320,128]{2,1,0:T(8,128)(2,1)} %get-tuple-element.36), channel_id=1, source_target_pairs={{0,252},{4,8},{8,4},{12,16},{16,12},{20,24},{24,20},{28,32},{32,28... | collective-permute-start | bytes 737288 | tf_op jit(solution)/shard_map/ppermute | solution.py:385
  25.2 1.0 %copy-done.3 = bf16[192,768]{1,0:T(8,128)(2,1)S(1)} copy-done((bf16[192,768]{1,0:T(8,128)(2,1)S(1)}, bf16[192,768]{1,0:T(8,128)(2,1)}, u32[]{:S(2)}) %copy-start.3) | copy-done | bytes 294936
  26.2 0.7 %cut.1 = (bf16[192,384]{1,0:T(8,128)(2,1)S(1)}, bf16[192,384]{1,0:T(8,128)(2,1)S(1)}) custom-call(bf16[192,768]{1,0:T(8,128)(2,1)S(1)} %copy-done.3, s32[1,4]{1,0:T(1,128)S(1)} %broadcast_in_dim.3.me), custom_call_target="tpu_custom_call" | custom-call | tf_op jit(solution)/shard_map/cut/pallas_call | solution.py:390
  26.9 1.2 %collective-permute-start.3 = (bf16[192,384]{1,0:T(8,128)(2,1)S(1)}, bf16[192,384]{1,0:T(8,128)(2,1)S(1)}, u32[]{:S(2)}, u32[]{:S(2)}) collective-permute-start(bf16[192,384]{1,0:T(8,128)(2,1)S(1)} %get-tuple-element.40), channel_id=1, source_target_pairs={{0,2},{1,3},{2,0},{3,1},{4,6},{5,7},{6,4},{7,5},{8,10},{9,11},{10,... | collective-permute-start | bytes 442376 | tf_op jit(solution)/shard_map/ppermute | solution.py:359
  28.1 1.0 %all-to-all-done = bf16[64,3,128]{2,1,0:T(4,128)(2,1)S(1)} async-done(((bf16[64,3,128]{2,1,0:T(4,128)(2,1)}), bf16[64,3,128]{2,1,0:T(4,128)(2,1)S(1)}, u32[]{:S(2)}, u32[]{:S(2)}) %all-to-all-start) | async-done | bytes 49184 | tf_op jit(solution)/shard_map/all_to_all | solution.py:386
  29.1 0.0 collective-permute-done.first_in
  29.1 0.0 copy-done.1
  29.2 0.0 copy-done
  29.2 0.0 copy-done.2
  29.2 2.7 %inner.1 = (f32[3,768,128]{2,1,0:T(8,128)S(1)}, f32[3,768,128]{2,1,0:T(8,128)S(1)}, bf16[3,512,128]{2,1,0:T(8,128)(2,1)S(1)}, bf16[3,512,128]{2,1,0:T(8,128)(2,1...) custom-call(bf16[3,512,128]{2,1,0:T(8,128)(2,1)S(1)} %bitcast.21, ...), custom_call_target="tpu_custom_call" | custom-call | flops 4000000000 | bytes 8000000 | tf_op jit(solution)/shard_map/inner/pallas_call | solution.py:401
  31.9 0.2 collective-permute-done.1.second_in
  32.1 1.5 %attend0.1 = bf16[1,512,128]{2,1,0:T(8,128)(2,1)S(1)} custom-call(bf16[3,512,128]{2,1,0:T(8,128)(2,1)S(1)} %bitcast.22, bf16[3,512,128]{2,1,0:T(8,128)(2,1)S(1)} %bitcast.13, bf16[3,512,128]{2,1,0:T(8,128)(2,1)S(1)} %bitcast.18, f32[3,768,128]{2,1,0:T(8,128)S(1)} %get-tuple-element.28.x0_in, f32[3,768,128]{2,1,0:T(8,128)S(1)} %get-tuple-element.29.m0_in, ...), custom_call_target="tpu_custom_call" | custom-call | tf_op jit(solution)/shard_map/attend0/pallas_call | solution.py:413
  33.6 1.2 %collective-permute-start.4 = (bf16[512,128]{1,0:T(8,128)(2,1)S(1)}, bf16[512,128]{1,0:T(8,128)(2,1)S(1)}, u32[]{:S(2)}, u32[]{:S(2)}) collective-permute-start(bf16[512,128]{1,0:T(8,128)(2,1)S(1)} %bitcast.28), channel_id=1, source_target_pairs={{0,2},{1,3},{2,0},{3,1},{4,6},{5,7},{6,4},{7,5},{8,10},{9,11},{10,... | collective-permute-start | bytes 393224 | tf_op jit(solution)/shard_map/ppermute | solution.py:359
  34.8 1.5 %attend1.1 = bf16[1,512,128]{2,1,0:T(8,128)(2,1)S(1)} custom-call(bf16[3,512,128]{2,1,0:T(8,128)(2,1)S(1)} %bitcast.23, bf16[3,512,128]{2,1,0:T(8,128)(2,1)S(1)} %bitcast.14, bf16[3,512,128]{2,1,0:T(8,128)(2,1)S(1)} %bitcast.19, f32[3,768,128]{2,1,0:T(8,128)S(1)} %get-tuple-element.28.x0_in, f32[3,768,128]{2,1,0:T(8,128)S(1)} %get-tuple-element.29.m0_in, ...), custom_call_target="tpu_custom_call" | custom-call | tf_op jit(solution)/shard_map/attend1/pallas_call | solution.py:413
  36.3 0.4 collective-permute-start.5
  36.7 1.5 %attend2.1 = bf16[1,512,128]{2,1,0:T(8,128)(2,1)S(1)} custom-call(bf16[3,512,128]{2,1,0:T(8,128)(2,1)S(1)} %bitcast.24, bf16[3,512,128]{2,1,0:T(8,128)(2,1)S(1)} %bitcast.15, bf16[3,512,128]{2,1,0:T(8,128)(2,1)S(1)} %bitcast.20, f32[3,768,128]{2,1,0:T(8,128)S(1)} %get-tuple-element.28.x0_in, f32[3,768,128]{2,1,0:T(8,128)S(1)} %get-tuple-element.29.m0_in, ...), custom_call_target="tpu_custom_call" | custom-call | tf_op jit(solution)/shard_map/attend2/pallas_call | solution.py:413
  38.1 1.2 %collective-permute-start.2 = (bf16[512,128]{1,0:T(8,128)(2,1)S(1)}, bf16[512,128]{1,0:T(8,128)(2,1)S(1)}, u32[]{:S(2)}, u32[]{:S(2)}) collective-permute-start(bf16[512,128]{1,0:T(8,128)(2,1)S(1)} %bitcast.32), channel_id=1, source_target_pairs={{0,2},{1,3},{2,0},{3,1},{4,6},{5,7},{6,4},{7,5},{8,10},{9,11},{10,... | collective-permute-start | bytes 393224 | tf_op jit(solution)/shard_map/ppermute | solution.py:359
  39.4 0.0 collective-permute-done.3.refs_6_.refs_2_
  39.4 0.0 collective-permute-done.4.refs_1_
  39.4 2.4 %collective-permute-done.5.refs_3_ = bf16[512,128]{1,0:T(8,128)(2,1)S(1)} collective-permute-done((bf16[512,128]{1,0:T(8,128)(2,1)S(1)}, bf16[512,128]{1,0:T(8,128)(2,1)S(1)}, u32[]{:S(2)}, u32[]{:S(2)}) %collective-permute-start.5) | collective-permute-done | bytes 131104 | tf_op jit(solution)/shard_map/ppermute | solution.py:359
  41.8 1.2 %project.2 = (f32[3,512,128]{2,1,0:T(8,128)S(1)}, f32[3,512,128]{2,1,0:T(8,128)S(1)}) custom-call(bf16[512,128]{1,0:T(8,128)(2,1)S(1)} %bitcast.29, bf16[512,128]{1,0:T(8,128)(2,1)S(1)} %collective-permute-done.4.refs_1_, bf16[512,128]{1,0:T(8,128)(2,1)S(1)} %bitcast.31, bf16[512,128]{1,0:T(8,128)(2,1)S(1)} %collective-permute-done.5.refs_3_, ...), custom_call_target="tpu_custom_call" | custom-call | tf_op jit(solution)/shard_map/project/pallas_call | solution.py:426
  43.1 1.3 %collective-permute-done.2.refs_0_ = bf16[512,128]{1,0:T(8,128)(2,1)S(1)} collective-permute-done((bf16[512,128]{1,0:T(8,128)(2,1)S(1)}, bf16[512,128]{1,0:T(8,128)(2,1)S(1)}, u32[]{:S(2)}, u32[]{:S(2)}) %collective-permute-start.2) | collective-permute-done | bytes 131104 | tf_op jit(solution)/shard_map/ppermute | solution.py:359
  44.4 0.4 project.3
  44.8 2.1 %collective-permute-start.6 = (bf16[3,512,128]{2,1,0:T(8,128)(2,1)S(1)}, bf16[3,512,128]{2,1,0:T(8,128)(2,1)S(1)}, u32[]{:S(2)}, u32[]{:S(2)}) collective-permute-start(bf16[3,512,128]{2,1,0:T(8,128)(2,1)S(1)} %get-tuple-element.44), channel_id=1, source_target_pairs={{0,1},{1,0},{2,3},{3,2},{4,5},{5,4},{6,7},{7,6},{8,9},{9,8},{10,11... | collective-permute-start | bytes 1179656 | tf_op jit(solution)/shard_map/ppermute | solution.py:359
  47.0 1.3 %collective-permute-done.6.other = bf16[3,512,128]{2,1,0:T(8,128)(2,1)S(1)} collective-permute-done((bf16[3,512,128]{2,1,0:T(8,128)(2,1)S(1)}, bf16[3,512,128]{2,1,0:T(8,128)(2,1)S(1)}, u32[]{:S(2)}, u32[]{:S(2)}) %collective-permute-start.6) | collective-permute-done | bytes 393248 | tf_op jit(solution)/shard_map/ppermute | solution.py:359
  48.3 0.8 %add.1 = bf16[3,512,128]{2,1,0:T(8,128)(2,1)} custom-call(f32[3,512,128]{2,1,0:T(8,128)S(1)} %get-tuple-element.43.mine, bf16[3,512,128]{2,1,0:T(8,128)(2,1)S(1)} %collective-permute-done.6.other), custom_call_target="tpu_custom_call" | custom-call | tf_op jit(solution)/shard_map/add/pallas_call | solution.py:434
  (3 shorter events, 0.0 us)
Async XLA Ops:
  0.0 29.1 %copy-start.1 = (bf16[512,3,128]{2,0,1:T(8,128)(2,1)S(1)}, bf16[512,3,128]{2,0,1:T(8,128)(2,1)}, u32[]{:S(2)}) copy-start(bf16[512,3,128]{2,0,1:T(8,128)(2,1)} %param.6) | copy-start | bytes 1179652
  0.0 29.1 %copy-start = (bf16[512,3,128]{2,0,1:T(8,128)(2,1)S(1)}, bf16[512,3,128]{2,0,1:T(8,128)(2,1)}, u32[]{:S(2)}) copy-start(bf16[512,3,128]{2,0,1:T(8,128)(2,1)} %param.5) | copy-start | bytes 1179652
  0.0 29.2 %copy-start.2 = (bf16[512,3,128]{2,0,1:T(8,128)(2,1)S(1)}, bf16[512,3,128]{2,0,1:T(8,128)(2,1)}, u32[]{:S(2)}) copy-start(bf16[512,3,128]{2,0,1:T(8,128)(2,1)} %param.4) | copy-start | bytes 1179652
  2.6 26.6 %collective-permute-start = (bf16[3,320,128]{2,1,0:T(8,128)(2,1)}, bf16[3,320,128]{2,1,0:T(8,128)(2,1)S(1)}, u32[]{:S(2)}, u32[]{:S(2)}) collective-permute-start(bf16[3,320,128]{2,1,0:T(8,128)(2,1)} %get-tuple-element.26), channel_id=1, source_target_pairs={{0,4},{4,0},{8,12},{12,8},{16,20},{20,16},{24,28},{28,24},{32,36},... | collective-permute-start | bytes 737288 | tf_op jit(solution)/shard_map/ppermute | solution.py:359
  6.2 22.9 %all-to-all-start = ((bf16[64,3,128]{2,1,0:T(4,128)(2,1)}), bf16[64,3,128]{2,1,0:T(4,128)(2,1)S(1)}, u32[]{:S(2)}, u32[]{:S(2)}) async-start(bf16[64,3,128]{2,1,0:T(4,128)(2,1)} %get-tuple-element.25), calls=%async_computation | async-start | bytes 131072 | tf_op jit(solution)/shard_map/all_to_all | solution.py:386
  18.1 14.0 %collective-permute-start.1 = (bf16[3,320,128]{2,1,0:T(8,128)(2,1)}, bf16[3,320,128]{2,1,0:T(8,128)(2,1)S(1)}, u32[]{:S(2)}, u32[]{:S(2)}) collective-permute-start(bf16[3,320,128]{2,1,0:T(8,128)(2,1)} %get-tuple-element.36), channel_id=1, source_target_pairs={{0,252},{4,8},{8,4},{12,16},{16,12},{20,24},{24,20},{28,32},{32,28... | collective-permute-start | bytes 737288 | tf_op jit(solution)/shard_map/ppermute | solution.py:385
  25.2 1.0 %copy-start.3 = (bf16[192,768]{1,0:T(8,128)(2,1)S(1)}, bf16[192,768]{1,0:T(8,128)(2,1)}, u32[]{:S(2)}) copy-start(bf16[192,768]{1,0:T(8,128)(2,1)} %w_ref) | copy-start | bytes 884740
  26.9 12.5 %collective-permute-start.3 = (bf16[192,384]{1,0:T(8,128)(2,1)S(1)}, bf16[192,384]{1,0:T(8,128)(2,1)S(1)}, u32[]{:S(2)}, u32[]{:S(2)}) collective-permute-start(bf16[192,384]{1,0:T(8,128)(2,1)S(1)} %get-tuple-element.40), channel_id=1, source_target_pairs={{0,2},{1,3},{2,0},{3,1},{4,6},{5,7},{6,4},{7,5},{8,10},{9,11},{10,... | collective-permute-start | bytes 442376 | tf_op jit(solution)/shard_map/ppermute | solution.py:359
  33.6 5.8 %collective-permute-start.4 = (bf16[512,128]{1,0:T(8,128)(2,1)S(1)}, bf16[512,128]{1,0:T(8,128)(2,1)S(1)}, u32[]{:S(2)}, u32[]{:S(2)}) collective-permute-start(bf16[512,128]{1,0:T(8,128)(2,1)S(1)} %bitcast.28), channel_id=1, source_target_pairs={{0,2},{1,3},{2,0},{3,1},{4,6},{5,7},{6,4},{7,5},{8,10},{9,11},{10,... | collective-permute-start | bytes 393224 | tf_op jit(solution)/shard_map/ppermute | solution.py:359
  36.3 5.5 %collective-permute-start.5 = (bf16[512,128]{1,0:T(8,128)(2,1)S(1)}, bf16[512,128]{1,0:T(8,128)(2,1)S(1)}, u32[]{:S(2)}, u32[]{:S(2)}) collective-permute-start(bf16[512,128]{1,0:T(8,128)(2,1)S(1)} %bitcast.30), channel_id=1, source_target_pairs={{0,2},{1,3},{2,0},{3,1},{4,6},{5,7},{6,4},{7,5},{8,10},{9,11},{10,... | collective-permute-start | bytes 393224 | tf_op jit(solution)/shard_map/ppermute | solution.py:359
  38.1 6.3 %collective-permute-start.2 = (bf16[512,128]{1,0:T(8,128)(2,1)S(1)}, bf16[512,128]{1,0:T(8,128)(2,1)S(1)}, u32[]{:S(2)}, u32[]{:S(2)}) collective-permute-start(bf16[512,128]{1,0:T(8,128)(2,1)S(1)} %bitcast.32), channel_id=1, source_target_pairs={{0,2},{1,3},{2,0},{3,1},{4,6},{5,7},{6,4},{7,5},{8,10},{9,11},{10,... | collective-permute-start | bytes 393224 | tf_op jit(solution)/shard_map/ppermute | solution.py:359
  44.8 3.5 %collective-permute-start.6 = (bf16[3,512,128]{2,1,0:T(8,128)(2,1)S(1)}, bf16[3,512,128]{2,1,0:T(8,128)(2,1)S(1)}, u32[]{:S(2)}, u32[]{:S(2)}) collective-permute-start(bf16[3,512,128]{2,1,0:T(8,128)(2,1)S(1)} %get-tuple-element.44), channel_id=1, source_target_pairs={{0,1},{1,0},{2,3},{3,2},{4,5},{5,4},{6,7},{7,6},{8,9},{9,8},{10,11... | collective-permute-start | bytes 1179656 | tf_op jit(solution)/shard_map/ppermute | solution.py:359

commit v2 on v1

--- a/solution.py
+++ b/solution.py
@@ -390,6 +390,7 @@
     w_own, w_far = pl.pallas_call(
         cut_kernel,
         in_specs=[vmem, pl.BlockSpec(memory_space=pltpu.SMEM)],
+        out_specs=[vmem] * 2,
         out_shape=[jax.ShapeDtypeStruct((w_out.shape[0], 2 * width), BF16)] * 2,
         compiler_params=params,
         name="cut",
@@ -413,6 +414,7 @@
         att = pl.pallas_call(
             functools.partial(attend_kernel, head),
             in_specs=[vmem] * 13 + [smem],
+            out_specs=vmem,
             out_shape=jax.ShapeDtypeStruct((1, rows, LANES), BF16),
             scratch_shapes=[pltpu.VMEM((6 * NR, LANES), BF16)] * 3 + [pltpu.VMEM((NR, LANES), F32)],
             compiler_params=params,

time: 49.3 us -> 49.3 us (level)
  no operation moved by 1% of the time
where the time goes in v2:
time: 49.3 us; the launch traced here: 49.1 us
  starting transfers between devices  28.9 us (59%)
  Pallas kernels  12.8 us (26%)
  waiting for transfers between devices  6.33 us (13%)
  local copies, waits for them, and re-layouts  0.98 us (2%)
    all_to_all x1, starting transfers between devices, on_device(): lax.all_to_all(top, 'seq', split_axis=0, concat_axis=0, tiled=True)  11.8 us
    ppermute x6, starting transfers between devices, exchange(): lax.ppermute(x, axis, [(i, i ^ bit) for i in range(lax.axis_size(axis))])  9.92 us
    ppermute x1, starting transfers between devices, on_device(): lax.ppermute(second_out, 'seq', [(i, (i - 1 if i % 2 == 0 else i + 1) % c...  7.13 us
    ppermute x6, waiting for transfers between devices, exchange(): lax.ppermute(x, axis, [(i, i ^ bit) for i in range(lax.axis_size(axis))])  5.13 us
    pallas_call x3, Pallas kernels, on_device(): pl.pallas_call(functools.partial(attend_kernel, head), in_specs=[vmem] *...  4.38 us
    pallas_call x1, Pallas kernels, on_device(): pl.pallas_call(inner_kernel, in_specs=[vmem] * 3, out_specs=[vmem] * 7, o...  2.69 us
    pallas_call x1, Pallas kernels, on_device(): pl.pallas_call(prepare_kernel, in_specs=[pl.BlockSpec(memory_space=pltpu....  2.54 us
    pallas_call x2, Pallas kernels, on_device(): pl.pallas_call(functools.partial(project_kernel, terms), in_specs=[vmem]...  1.66 us
  transfers between devices with their start and end apart: 8, of which 5 were waited for; matrix products, arithmetic and copies ran while one was open for 0% of the time, Pallas kernels for 18%

profile of v2, /device:TPU:1, one launch (start us, length us, event | category | flops | bytes accessed | tf_op | source)
XLA Modules:
  0.0 49.1 jit_solution(14308281085764093166)
XLA Ops:
  0.0 0.0 copy-start.1
  0.0 0.0 copy-start
  0.0 0.0 copy-start.2
  0.0 2.5 %prepare.1 = (bf16[64,3,128]{2,1,0:T(4,128)(2,1)}, bf16[3,320,128]{2,1,0:T(8,128)(2,1)}, bf16[3,320,128]{2,1,0:T(8,128)(2,1)}) custom-call(bf16[3,512,128]{2,1,0:T(8,128)(2,1)} %bitcast.11, bf16[3,512,128]{2,1,0:T(8,128)(2,1)} %bitcast.16, s32[1]{0:T(128)} %bitcast.2.place), custom_call_target="tpu_custom_call" | custom-call | tf_op jit(solution)/shard_map/prepare/pallas_call | solution.py:374
  2.6 3.7 %collective-permute-start = (bf16[3,320,128]{2,1,0:T(8,128)(2,1)}, bf16[3,320,128]{2,1,0:T(8,128)(2,1)S(1)}, u32[]{:S(2)}, u32[]{:S(2)}) collective-permute-start(bf16[3,320,128]{2,1,0:T(8,128)(2,1)} %get-tuple-element.26), channel_id=1, source_target_pairs={{0,4},{4,0},{8,12},{12,8},{16,20},{20,16},{24,28},{28,24},{32,36},... | collective-permute-start | bytes 737288 | tf_op jit(solution)/shard_map/ppermute | solution.py:359
  6.2 11.8 %all-to-all-start = ((bf16[64,3,128]{2,1,0:T(4,128)(2,1)}), bf16[64,3,128]{2,1,0:T(4,128)(2,1)S(1)}, u32[]{:S(2)}, u32[]{:S(2)}) async-start(bf16[64,3,128]{2,1,0:T(4,128)(2,1)} %get-tuple-element.25), calls=%async_computation | async-start | bytes 131072 | tf_op jit(solution)/shard_map/all_to_all | solution.py:386
  18.1 7.1 %collective-permute-start.1 = (bf16[3,320,128]{2,1,0:T(8,128)(2,1)}, bf16[3,320,128]{2,1,0:T(8,128)(2,1)S(1)}, u32[]{:S(2)}, u32[]{:S(2)}) collective-permute-start(bf16[3,320,128]{2,1,0:T(8,128)(2,1)} %get-tuple-element.36), channel_id=1, source_target_pairs={{0,252},{4,8},{8,4},{12,16},{16,12},{20,24},{24,20},{28,32},{32,28... | collective-permute-start | bytes 737288 | tf_op jit(solution)/shard_map/ppermute | solution.py:385
  25.2 1.0 %copy-done.3 = bf16[192,768]{1,0:T(8,128)(2,1)S(1)} copy-done((bf16[192,768]{1,0:T(8,128)(2,1)S(1)}, bf16[192,768]{1,0:T(8,128)(2,1)}, u32[]{:S(2)}) %copy-start.3) | copy-done | bytes 294936
  26.2 0.7 %cut.1 = (bf16[192,384]{1,0:T(8,128)(2,1)S(1)}, bf16[192,384]{1,0:T(8,128)(2,1)S(1)}) custom-call(bf16[192,768]{1,0:T(8,128)(2,1)S(1)} %copy-done.3, s32[1,4]{1,0:T(1,128)S(1)} %broadcast_in_dim.3.me), custom_call_target="tpu_custom_call" | custom-call | tf_op jit(solution)/shard_map/cut/pallas_call | solution.py:390
  26.9 1.2 %collective-permute-start.3 = (bf16[192,384]{1,0:T(8,128)(2,1)S(1)}, bf16[192,384]{1,0:T(8,128)(2,1)S(1)}, u32[]{:S(2)}, u32[]{:S(2)}) collective-permute-start(bf16[192,384]{1,0:T(8,128)(2,1)S(1)} %get-tuple-element.40), channel_id=1, source_target_pairs={{0,2},{1,3},{2,0},{3,1},{4,6},{5,7},{6,4},{7,5},{8,10},{9,11},{10,... | collective-permute-start | bytes 442376 | tf_op jit(solution)/shard_map/ppermute | solution.py:359
  28.1 1.0 %all-to-all-done = bf16[64,3,128]{2,1,0:T(4,128)(2,1)S(1)} async-done(((bf16[64,3,128]{2,1,0:T(4,128)(2,1)}), bf16[64,3,128]{2,1,0:T(4,128)(2,1)S(1)}, u32[]{:S(2)}, u32[]{:S(2)}) %all-to-all-start) | async-done | bytes 49184 | tf_op jit(solution)/shard_map/all_to_all | solution.py:386
  29.1 0.0 collective-permute-done.first_in
  29.1 0.0 copy-done.1
  29.2 0.0 copy-done
  29.2 0.0 copy-done.2
  29.2 2.7 %inner.1 = (f32[3,768,128]{2,1,0:T(8,128)S(1)}, f32[3,768,128]{2,1,0:T(8,128)S(1)}, bf16[3,512,128]{2,1,0:T(8,128)(2,1)S(1)}, bf16[3,512,128]{2,1,0:T(8,128)(2,1...) custom-call(bf16[3,512,128]{2,1,0:T(8,128)(2,1)S(1)} %bitcast.21, ...), custom_call_target="tpu_custom_call" | custom-call | flops 4000000000 | bytes 8000000 | tf_op jit(solution)/shard_map/inner/pallas_call | solution.py:402
  31.9 0.2 collective-permute-done.1.second_in
  32.1 1.5 %attend0.1 = bf16[1,512,128]{2,1,0:T(8,128)(2,1)S(1)} custom-call(bf16[3,512,128]{2,1,0:T(8,128)(2,1)S(1)} %bitcast.22, bf16[3,512,128]{2,1,0:T(8,128)(2,1)S(1)} %bitcast.13, bf16[3,512,128]{2,1,0:T(8,128)(2,1)S(1)} %bitcast.18, f32[3,768,128]{2,1,0:T(8,128)S(1)} %get-tuple-element.28.x0_in, f32[3,768,128]{2,1,0:T(8,128)S(1)} %get-tuple-element.29.m0_in, ...), custom_call_target="tpu_custom_call" | custom-call | tf_op jit(solution)/shard_map/attend0/pallas_call | solution.py:414
  33.6 1.2 %collective-permute-start.4 = (bf16[512,128]{1,0:T(8,128)(2,1)S(1)}, bf16[512,128]{1,0:T(8,128)(2,1)S(1)}, u32[]{:S(2)}, u32[]{:S(2)}) collective-permute-start(bf16[512,128]{1,0:T(8,128)(2,1)S(1)} %bitcast.28), channel_id=1, source_target_pairs={{0,2},{1,3},{2,0},{3,1},{4,6},{5,7},{6,4},{7,5},{8,10},{9,11},{10,... | collective-permute-start | bytes 393224 | tf_op jit(solution)/shard_map/ppermute | solution.py:359
  34.8 1.5 %attend1.1 = bf16[1,512,128]{2,1,0:T(8,128)(2,1)S(1)} custom-call(bf16[3,512,128]{2,1,0:T(8,128)(2,1)S(1)} %bitcast.23, bf16[3,512,128]{2,1,0:T(8,128)(2,1)S(1)} %bitcast.14, bf16[3,512,128]{2,1,0:T(8,128)(2,1)S(1)} %bitcast.19, f32[3,768,128]{2,1,0:T(8,128)S(1)} %get-tuple-element.28.x0_in, f32[3,768,128]{2,1,0:T(8,128)S(1)} %get-tuple-element.29.m0_in, ...), custom_call_target="tpu_custom_call" | custom-call | tf_op jit(solution)/shard_map/attend1/pallas_call | solution.py:414
  36.3 0.4 collective-permute-start.5
  36.7 1.5 %attend2.1 = bf16[1,512,128]{2,1,0:T(8,128)(2,1)S(1)} custom-call(bf16[3,512,128]{2,1,0:T(8,128)(2,1)S(1)} %bitcast.24, bf16[3,512,128]{2,1,0:T(8,128)(2,1)S(1)} %bitcast.15, bf16[3,512,128]{2,1,0:T(8,128)(2,1)S(1)} %bitcast.20, f32[3,768,128]{2,1,0:T(8,128)S(1)} %get-tuple-element.28.x0_in, f32[3,768,128]{2,1,0:T(8,128)S(1)} %get-tuple-element.29.m0_in, ...), custom_call_target="tpu_custom_call" | custom-call | tf_op jit(solution)/shard_map/attend2/pallas_call | solution.py:414
  38.1 1.2 %collective-permute-start.2 = (bf16[512,128]{1,0:T(8,128)(2,1)S(1)}, bf16[512,128]{1,0:T(8,128)(2,1)S(1)}, u32[]{:S(2)}, u32[]{:S(2)}) collective-permute-start(bf16[512,128]{1,0:T(8,128)(2,1)S(1)} %bitcast.32), channel_id=1, source_target_pairs={{0,2},{1,3},{2,0},{3,1},{4,6},{5,7},{6,4},{7,5},{8,10},{9,11},{10,... | collective-permute-start | bytes 393224 | tf_op jit(solution)/shard_map/ppermute | solution.py:359
  39.4 0.0 collective-permute-done.3.refs_6_.refs_2_
  39.4 0.0 collective-permute-done.4.refs_1_
  39.4 2.4 %collective-permute-done.5.refs_3_ = bf16[512,128]{1,0:T(8,128)(2,1)S(1)} collective-permute-done((bf16[512,128]{1,0:T(8,128)(2,1)S(1)}, bf16[512,128]{1,0:T(8,128)(2,1)S(1)}, u32[]{:S(2)}, u32[]{:S(2)}) %collective-permute-start.5) | collective-permute-done | bytes 131104 | tf_op jit(solution)/shard_map/ppermute | solution.py:359
  41.8 1.2 %project.2 = (f32[3,512,128]{2,1,0:T(8,128)S(1)}, f32[3,512,128]{2,1,0:T(8,128)S(1)}) custom-call(bf16[512,128]{1,0:T(8,128)(2,1)S(1)} %bitcast.29, bf16[512,128]{1,0:T(8,128)(2,1)S(1)} %collective-permute-done.4.refs_1_, bf16[512,128]{1,0:T(8,128)(2,1)S(1)} %bitcast.31, bf16[512,128]{1,0:T(8,128)(2,1)S(1)} %collective-permute-done.5.refs_3_, ...), custom_call_target="tpu_custom_call" | custom-call | tf_op jit(solution)/shard_map/project/pallas_call | solution.py:428
  43.1 1.3 %collective-permute-done.2.refs_0_ = bf16[512,128]{1,0:T(8,128)(2,1)S(1)} collective-permute-done((bf16[512,128]{1,0:T(8,128)(2,1)S(1)}, bf16[512,128]{1,0:T(8,128)(2,1)S(1)}, u32[]{:S(2)}, u32[]{:S(2)}) %collective-permute-start.2) | collective-permute-done | bytes 131104 | tf_op jit(solution)/shard_map/ppermute | solution.py:359
  44.4 0.4 project.3
  44.8 2.1 %collective-permute-start.6 = (bf16[3,512,128]{2,1,0:T(8,128)(2,1)S(1)}, bf16[3,512,128]{2,1,0:T(8,128)(2,1)S(1)}, u32[]{:S(2)}, u32[]{:S(2)}) collective-permute-start(bf16[3,512,128]{2,1,0:T(8,128)(2,1)S(1)} %get-tuple-element.44), channel_id=1, source_target_pairs={{0,1},{1,0},{2,3},{3,2},{4,5},{5,4},{6,7},{7,6},{8,9},{9,8},{10,11... | collective-permute-start | bytes 1179656 | tf_op jit(solution)/shard_map/ppermute | solution.py:359
  47.0 1.3 %collective-permute-done.6.other = bf16[3,512,128]{2,1,0:T(8,128)(2,1)S(1)} collective-permute-done((bf16[3,512,128]{2,1,0:T(8,128)(2,1)S(1)}, bf16[3,512,128]{2,1,0:T(8,128)(2,1)S(1)}, u32[]{:S(2)}, u32[]{:S(2)}) %collective-permute-start.6) | collective-permute-done | bytes 393248 | tf_op jit(solution)/shard_map/ppermute | solution.py:359
  48.3 0.8 %add.1 = bf16[3,512,128]{2,1,0:T(8,128)(2,1)} custom-call(f32[3,512,128]{2,1,0:T(8,128)S(1)} %get-tuple-element.43.mine, bf16[3,512,128]{2,1,0:T(8,128)(2,1)S(1)} %collective-permute-done.6.other), custom_call_target="tpu_custom_call" | custom-call | tf_op jit(solution)/shard_map/add/pallas_call | solution.py:436
  (3 shorter events, 0.0 us)
Async XLA Ops:
  0.0 29.1 %copy-start.1 = (bf16[512,3,128]{2,0,1:T(8,128)(2,1)S(1)}, bf16[512,3,128]{2,0,1:T(8,128)(2,1)}, u32[]{:S(2)}) copy-start(bf16[512,3,128]{2,0,1:T(8,128)(2,1)} %param.6) | copy-start | bytes 1179652
  0.0 29.1 %copy-start = (bf16[512,3,128]{2,0,1:T(8,128)(2,1)S(1)}, bf16[512,3,128]{2,0,1:T(8,128)(2,1)}, u32[]{:S(2)}) copy-start(bf16[512,3,128]{2,0,1:T(8,128)(2,1)} %param.5) | copy-start | bytes 1179652
  0.0 29.2 %copy-start.2 = (bf16[512,3,128]{2,0,1:T(8,128)(2,1)S(1)}, bf16[512,3,128]{2,0,1:T(8,128)(2,1)}, u32[]{:S(2)}) copy-start(bf16[512,3,128]{2,0,1:T(8,128)(2,1)} %param.4) | copy-start | bytes 1179652
  2.6 26.6 %collective-permute-start = (bf16[3,320,128]{2,1,0:T(8,128)(2,1)}, bf16[3,320,128]{2,1,0:T(8,128)(2,1)S(1)}, u32[]{:S(2)}, u32[]{:S(2)}) collective-permute-start(bf16[3,320,128]{2,1,0:T(8,128)(2,1)} %get-tuple-element.26), channel_id=1, source_target_pairs={{0,4},{4,0},{8,12},{12,8},{16,20},{20,16},{24,28},{28,24},{32,36},... | collective-permute-start | bytes 737288 | tf_op jit(solution)/shard_map/ppermute | solution.py:359
  6.2 22.9 %all-to-all-start = ((bf16[64,3,128]{2,1,0:T(4,128)(2,1)}), bf16[64,3,128]{2,1,0:T(4,128)(2,1)S(1)}, u32[]{:S(2)}, u32[]{:S(2)}) async-start(bf16[64,3,128]{2,1,0:T(4,128)(2,1)} %get-tuple-element.25), calls=%async_computation | async-start | bytes 131072 | tf_op jit(solution)/shard_map/all_to_all | solution.py:386
  18.1 14.0 %collective-permute-start.1 = (bf16[3,320,128]{2,1,0:T(8,128)(2,1)}, bf16[3,320,128]{2,1,0:T(8,128)(2,1)S(1)}, u32[]{:S(2)}, u32[]{:S(2)}) collective-permute-start(bf16[3,320,128]{2,1,0:T(8,128)(2,1)} %get-tuple-element.36), channel_id=1, source_target_pairs={{0,252},{4,8},{8,4},{12,16},{16,12},{20,24},{24,20},{28,32},{32,28... | collective-permute-start | bytes 737288 | tf_op jit(solution)/shard_map/ppermute | solution.py:385
  25.2 1.0 %copy-start.3 = (bf16[192,768]{1,0:T(8,128)(2,1)S(1)}, bf16[192,768]{1,0:T(8,128)(2,1)}, u32[]{:S(2)}) copy-start(bf16[192,768]{1,0:T(8,128)(2,1)} %w_ref) | copy-start | bytes 884740
  26.9 12.5 %collective-permute-start.3 = (bf16[192,384]{1,0:T(8,128)(2,1)S(1)}, bf16[192,384]{1,0:T(8,128)(2,1)S(1)}, u32[]{:S(2)}, u32[]{:S(2)}) collective-permute-start(bf16[192,384]{1,0:T(8,128)(2,1)S(1)} %get-tuple-element.40), channel_id=1, source_target_pairs={{0,2},{1,3},{2,0},{3,1},{4,6},{5,7},{6,4},{7,5},{8,10},{9,11},{10,... | collective-permute-start | bytes 442376 | tf_op jit(solution)/shard_map/ppermute | solution.py:359
  33.6 5.8 %collective-permute-start.4 = (bf16[512,128]{1,0:T(8,128)(2,1)S(1)}, bf16[512,128]{1,0:T(8,128)(2,1)S(1)}, u32[]{:S(2)}, u32[]{:S(2)}) collective-permute-start(bf16[512,128]{1,0:T(8,128)(2,1)S(1)} %bitcast.28), channel_id=1, source_target_pairs={{0,2},{1,3},{2,0},{3,1},{4,6},{5,7},{6,4},{7,5},{8,10},{9,11},{10,... | collective-permute-start | bytes 393224 | tf_op jit(solution)/shard_map/ppermute | solution.py:359
  36.3 5.5 %collective-permute-start.5 = (bf16[512,128]{1,0:T(8,128)(2,1)S(1)}, bf16[512,128]{1,0:T(8,128)(2,1)S(1)}, u32[]{:S(2)}, u32[]{:S(2)}) collective-permute-start(bf16[512,128]{1,0:T(8,128)(2,1)S(1)} %bitcast.30), channel_id=1, source_target_pairs={{0,2},{1,3},{2,0},{3,1},{4,6},{5,7},{6,4},{7,5},{8,10},{9,11},{10,... | collective-permute-start | bytes 393224 | tf_op jit(solution)/shard_map/ppermute | solution.py:359
  38.1 6.3 %collective-permute-start.2 = (bf16[512,128]{1,0:T(8,128)(2,1)S(1)}, bf16[512,128]{1,0:T(8,128)(2,1)S(1)}, u32[]{:S(2)}, u32[]{:S(2)}) collective-permute-start(bf16[512,128]{1,0:T(8,128)(2,1)S(1)} %bitcast.32), channel_id=1, source_target_pairs={{0,2},{1,3},{2,0},{3,1},{4,6},{5,7},{6,4},{7,5},{8,10},{9,11},{10,... | collective-permute-start | bytes 393224 | tf_op jit(solution)/shard_map/ppermute | solution.py:359
  44.8 3.5 %collective-permute-start.6 = (bf16[3,512,128]{2,1,0:T(8,128)(2,1)S(1)}, bf16[3,512,128]{2,1,0:T(8,128)(2,1)S(1)}, u32[]{:S(2)}, u32[]{:S(2)}) collective-permute-start(bf16[3,512,128]{2,1,0:T(8,128)(2,1)S(1)} %get-tuple-element.44), channel_id=1, source_target_pairs={{0,1},{1,0},{2,3},{3,2},{4,5},{5,4},{6,7},{7,6},{8,9},{9,8},{10,11... | collective-permute-start | bytes 1179656 | tf_op jit(solution)/shard_map/ppermute | solution.py:359

commit v3 on v2

--- a/solution.py
+++ b/solution.py
@@ -124,9 +124,9 @@
 
 def run_stages(stages, blocks):
     held = [{} for _ in stages]
-    for step in range(len(blocks) + 2 * len(stages)):
+    for step in range(len(blocks) + 3 * len(stages)):
         for index, stage in enumerate(stages):
-            at = step - 2 * index
+            at = step - 3 * index
             if 0 <= at < len(blocks):
                 given = held[index - 1].pop(at) if index else ()
                 held[index][at] = stage(blocks[at], *given)

time: 49.3 us -> 49.2 us (level)
  no operation moved by 1% of the time
where the time goes in v3:
time: 49.2 us; the launch traced here: 49 us
  starting transfers between devices  28.9 us (59%)
  Pallas kernels  12.8 us (26%)
  waiting for transfers between devices  6.17 us (13%)
  local copies, waits for them, and re-layouts  0.98 us (2%)
    all_to_all x1, starting transfers between devices, on_device(): lax.all_to_all(top, 'seq', split_axis=0, concat_axis=0, tiled=True)  11.8 us
    ppermute x6, starting transfers between devices, exchange(): lax.ppermute(x, axis, [(i, i ^ bit) for i in range(lax.axis_size(axis))])  9.97 us
    ppermute x1, starting transfers between devices, on_device(): lax.ppermute(second_out, 'seq', [(i, (i - 1 if i % 2 == 0 else i + 1) % c...  7.13 us
    ppermute x6, waiting for transfers between devices, exchange(): lax.ppermute(x, axis, [(i, i ^ bit) for i in range(lax.axis_size(axis))])  4.83 us
    pallas_call x3, Pallas kernels, on_device(): pl.pallas_call(functools.partial(attend_kernel, head), in_specs=[vmem] *...  4.54 us
    pallas_call x1, Pallas kernels, on_device(): pl.pallas_call(inner_kernel, in_specs=[vmem] * 3, out_specs=[vmem] * 7, o...  2.55 us
    pallas_call x1, Pallas kernels, on_device(): pl.pallas_call(prepare_kernel, in_specs=[pl.BlockSpec(memory_space=pltpu....  2.54 us
    pallas_call x2, Pallas kernels, on_device(): pl.pallas_call(functools.partial(project_kernel, terms), in_specs=[vmem]...  1.66 us
  transfers between devices with their start and end apart: 8, of which 5 were waited for; matrix products, arithmetic and copies ran while one was open for 0% of the time, Pallas kernels for 18%

profile of v3, /device:TPU:1, one launch (start us, length us, event | category | flops | bytes accessed | tf_op | source)
XLA Modules:
  0.0 49.0 jit_solution(13675300671427623162)
XLA Ops:
  0.0 0.0 copy-start.1
  0.0 0.0 copy-start
  0.0 0.0 copy-start.2
  0.0 2.5 %prepare.1 = (bf16[64,3,128]{2,1,0:T(4,128)(2,1)}, bf16[3,320,128]{2,1,0:T(8,128)(2,1)}, bf16[3,320,128]{2,1,0:T(8,128)(2,1)}) custom-call(bf16[3,512,128]{2,1,0:T(8,128)(2,1)} %bitcast.11, bf16[3,512,128]{2,1,0:T(8,128)(2,1)} %bitcast.16, s32[1]{0:T(128)} %bitcast.2.place), custom_call_target="tpu_custom_call" | custom-call | tf_op jit(solution)/shard_map/prepare/pallas_call | solution.py:374
  2.6 3.7 %collective-permute-start = (bf16[3,320,128]{2,1,0:T(8,128)(2,1)}, bf16[3,320,128]{2,1,0:T(8,128)(2,1)S(1)}, u32[]{:S(2)}, u32[]{:S(2)}) collective-permute-start(bf16[3,320,128]{2,1,0:T(8,128)(2,1)} %get-tuple-element.26), channel_id=1, source_target_pairs={{0,4},{4,0},{8,12},{12,8},{16,20},{20,16},{24,28},{28,24},{32,36},... | collective-permute-start | bytes 737288 | tf_op jit(solution)/shard_map/ppermute | solution.py:359
  6.2 11.8 %all-to-all-start = ((bf16[64,3,128]{2,1,0:T(4,128)(2,1)}), bf16[64,3,128]{2,1,0:T(4,128)(2,1)S(1)}, u32[]{:S(2)}, u32[]{:S(2)}) async-start(bf16[64,3,128]{2,1,0:T(4,128)(2,1)} %get-tuple-element.25), calls=%async_computation | async-start | bytes 131072 | tf_op jit(solution)/shard_map/all_to_all | solution.py:386
  18.1 7.1 %collective-permute-start.1 = (bf16[3,320,128]{2,1,0:T(8,128)(2,1)}, bf16[3,320,128]{2,1,0:T(8,128)(2,1)S(1)}, u32[]{:S(2)}, u32[]{:S(2)}) collective-permute-start(bf16[3,320,128]{2,1,0:T(8,128)(2,1)} %get-tuple-element.36), channel_id=1, source_target_pairs={{0,252},{4,8},{8,4},{12,16},{16,12},{20,24},{24,20},{28,32},{32,28... | collective-permute-start | bytes 737288 | tf_op jit(solution)/shard_map/ppermute | solution.py:385
  25.2 1.0 %copy-done.3 = bf16[192,768]{1,0:T(8,128)(2,1)S(1)} copy-done((bf16[192,768]{1,0:T(8,128)(2,1)S(1)}, bf16[192,768]{1,0:T(8,128)(2,1)}, u32[]{:S(2)}) %copy-start.3) | copy-done | bytes 294936
  26.2 0.7 %cut.1 = (bf16[192,384]{1,0:T(8,128)(2,1)S(1)}, bf16[192,384]{1,0:T(8,128)(2,1)S(1)}) custom-call(bf16[192,768]{1,0:T(8,128)(2,1)S(1)} %copy-done.3, s32[1,4]{1,0:T(1,128)S(1)} %broadcast_in_dim.3.me), custom_call_target="tpu_custom_call" | custom-call | tf_op jit(solution)/shard_map/cut/pallas_call | solution.py:390
  26.9 1.2 %collective-permute-start.3 = (bf16[192,384]{1,0:T(8,128)(2,1)S(1)}, bf16[192,384]{1,0:T(8,128)(2,1)S(1)}, u32[]{:S(2)}, u32[]{:S(2)}) collective-permute-start(bf16[192,384]{1,0:T(8,128)(2,1)S(1)} %get-tuple-element.40), channel_id=1, source_target_pairs={{0,2},{1,3},{2,0},{3,1},{4,6},{5,7},{6,4},{7,5},{8,10},{9,11},{10,... | collective-permute-start | bytes 442376 | tf_op jit(solution)/shard_map/ppermute | solution.py:359
  28.1 1.0 %all-to-all-done = bf16[64,3,128]{2,1,0:T(4,128)(2,1)S(1)} async-done(((bf16[64,3,128]{2,1,0:T(4,128)(2,1)}), bf16[64,3,128]{2,1,0:T(4,128)(2,1)S(1)}, u32[]{:S(2)}, u32[]{:S(2)}) %all-to-all-start) | async-done | bytes 49184 | tf_op jit(solution)/shard_map/all_to_all | solution.py:386
  29.1 0.0 collective-permute-done.first_in
  29.1 0.0 copy-done.1
  29.2 0.0 copy-done
  29.2 0.0 copy-done.2
  29.2 2.5 %inner.1 = (f32[3,768,128]{2,1,0:T(8,128)S(1)}, f32[3,768,128]{2,1,0:T(8,128)S(1)}, bf16[3,512,128]{2,1,0:T(8,128)(2,1)S(1)}, bf16[3,512,128]{2,1,0:T(8,128)(2,1...) custom-call(bf16[3,512,128]{2,1,0:T(8,128)(2,1)S(1)} %bitcast.21, ...), custom_call_target="tpu_custom_call" | custom-call | flops 4000000000 | bytes 8000000 | tf_op jit(solution)/shard_map/inner/pallas_call | solution.py:402
  31.7 0.4 collective-permute-done.1.second_in
  32.1 1.5 %attend0.1 = bf16[1,512,128]{2,1,0:T(8,128)(2,1)S(1)} custom-call(bf16[3,512,128]{2,1,0:T(8,128)(2,1)S(1)} %bitcast.22, bf16[3,512,128]{2,1,0:T(8,128)(2,1)S(1)} %bitcast.13, bf16[3,512,128]{2,1,0:T(8,128)(2,1)S(1)} %bitcast.18, f32[3,768,128]{2,1,0:T(8,128)S(1)} %get-tuple-element.28.x0_in, f32[3,768,128]{2,1,0:T(8,128)S(1)} %get-tuple-element.29.m0_in, ...), custom_call_target="tpu_custom_call" | custom-call | tf_op jit(solution)/shard_map/attend0/pallas_call | solution.py:414
  33.6 1.2 %collective-permute-start.4 = (bf16[512,128]{1,0:T(8,128)(2,1)S(1)}, bf16[512,128]{1,0:T(8,128)(2,1)S(1)}, u32[]{:S(2)}, u32[]{:S(2)}) collective-permute-start(bf16[512,128]{1,0:T(8,128)(2,1)S(1)} %bitcast.28), channel_id=1, source_target_pairs={{0,2},{1,3},{2,0},{3,1},{4,6},{5,7},{6,4},{7,5},{8,10},{9,11},{10,... | collective-permute-start | bytes 393224 | tf_op jit(solution)/shard_map/ppermute | solution.py:359
  34.8 1.5 %attend1.1 = bf16[1,512,128]{2,1,0:T(8,128)(2,1)S(1)} custom-call(bf16[3,512,128]{2,1,0:T(8,128)(2,1)S(1)} %bitcast.23, bf16[3,512,128]{2,1,0:T(8,128)(2,1)S(1)} %bitcast.14, bf16[3,512,128]{2,1,0:T(8,128)(2,1)S(1)} %bitcast.19, f32[3,768,128]{2,1,0:T(8,128)S(1)} %get-tuple-element.28.x0_in, f32[3,768,128]{2,1,0:T(8,128)S(1)} %get-tuple-element.29.m0_in, ...), custom_call_target="tpu_custom_call" | custom-call | tf_op jit(solution)/shard_map/attend1/pallas_call | solution.py:414
  36.4 0.4 collective-permute-start.5
  36.8 1.5 %attend2.1 = bf16[1,512,128]{2,1,0:T(8,128)(2,1)S(1)} custom-call(bf16[3,512,128]{2,1,0:T(8,128)(2,1)S(1)} %bitcast.24, bf16[3,512,128]{2,1,0:T(8,128)(2,1)S(1)} %bitcast.15, bf16[3,512,128]{2,1,0:T(8,128)(2,1)S(1)} %bitcast.20, f32[3,768,128]{2,1,0:T(8,128)S(1)} %get-tuple-element.28.x0_in, f32[3,768,128]{2,1,0:T(8,128)S(1)} %get-tuple-element.29.m0_in, ...), custom_call_target="tpu_custom_call" | custom-call | tf_op jit(solution)/shard_map/attend2/pallas_call | solution.py:414
  38.3 1.2 %collective-permute-start.2 = (bf16[512,128]{1,0:T(8,128)(2,1)S(1)}, bf16[512,128]{1,0:T(8,128)(2,1)S(1)}, u32[]{:S(2)}, u32[]{:S(2)}) collective-permute-start(bf16[512,128]{1,0:T(8,128)(2,1)S(1)} %bitcast.32), channel_id=1, source_target_pairs={{0,2},{1,3},{2,0},{3,1},{4,6},{5,7},{6,4},{7,5},{8,10},{9,11},{10,... | collective-permute-start | bytes 393224 | tf_op jit(solution)/shard_map/ppermute | solution.py:359
  39.5 0.0 collective-permute-done.3.refs_6_.refs_2_
  39.5 0.0 collective-permute-done.4.refs_1_
  39.5 2.0 %collective-permute-done.5.refs_3_ = bf16[512,128]{1,0:T(8,128)(2,1)S(1)} collective-permute-done((bf16[512,128]{1,0:T(8,128)(2,1)S(1)}, bf16[512,128]{1,0:T(8,128)(2,1)S(1)}, u32[]{:S(2)}, u32[]{:S(2)}) %collective-permute-start.5) | collective-permute-done | bytes 131104 | tf_op jit(solution)/shard_map/ppermute | solution.py:359
  41.5 1.2 %project.2 = (f32[3,512,128]{2,1,0:T(8,128)S(1)}, f32[3,512,128]{2,1,0:T(8,128)S(1)}) custom-call(bf16[512,128]{1,0:T(8,128)(2,1)S(1)} %bitcast.29, bf16[512,128]{1,0:T(8,128)(2,1)S(1)} %collective-permute-done.4.refs_1_, bf16[512,128]{1,0:T(8,128)(2,1)S(1)} %bitcast.31, bf16[512,128]{1,0:T(8,128)(2,1)S(1)} %collective-permute-done.5.refs_3_, ...), custom_call_target="tpu_custom_call" | custom-call | tf_op jit(solution)/shard_map/project/pallas_call | solution.py:428
  42.8 1.5 %collective-permute-done.2.refs_0_ = bf16[512,128]{1,0:T(8,128)(2,1)S(1)} collective-permute-done((bf16[512,128]{1,0:T(8,128)(2,1)S(1)}, bf16[512,128]{1,0:T(8,128)(2,1)S(1)}, u32[]{:S(2)}, u32[]{:S(2)}) %collective-permute-start.2) | collective-permute-done | bytes 131104 | tf_op jit(solution)/shard_map/ppermute | solution.py:359
  44.3 0.4 project.3
  44.7 2.2 %collective-permute-start.6 = (bf16[3,512,128]{2,1,0:T(8,128)(2,1)S(1)}, bf16[3,512,128]{2,1,0:T(8,128)(2,1)S(1)}, u32[]{:S(2)}, u32[]{:S(2)}) collective-permute-start(bf16[3,512,128]{2,1,0:T(8,128)(2,1)S(1)} %get-tuple-element.44), channel_id=1, source_target_pairs={{0,1},{1,0},{2,3},{3,2},{4,5},{5,4},{6,7},{7,6},{8,9},{9,8},{10,11... | collective-permute-start | bytes 1179656 | tf_op jit(solution)/shard_map/ppermute | solution.py:359
  46.9 1.3 %collective-permute-done.6.other = bf16[3,512,128]{2,1,0:T(8,128)(2,1)S(1)} collective-permute-done((bf16[3,512,128]{2,1,0:T(8,128)(2,1)S(1)}, bf16[3,512,128]{2,1,0:T(8,128)(2,1)S(1)}, u32[]{:S(2)}, u32[]{:S(2)}) %collective-permute-start.6) | collective-permute-done | bytes 393248 | tf_op jit(solution)/shard_map/ppermute | solution.py:359
  48.2 0.8 %add.1 = bf16[3,512,128]{2,1,0:T(8,128)(2,1)} custom-call(f32[3,512,128]{2,1,0:T(8,128)S(1)} %get-tuple-element.43.mine, bf16[3,512,128]{2,1,0:T(8,128)(2,1)S(1)} %collective-permute-done.6.other), custom_call_target="tpu_custom_call" | custom-call | tf_op jit(solution)/shard_map/add/pallas_call | solution.py:436
  (3 shorter events, 0.0 us)
Async XLA Ops:
  0.0 29.1 %copy-start.1 = (bf16[512,3,128]{2,0,1:T(8,128)(2,1)S(1)}, bf16[512,3,128]{2,0,1:T(8,128)(2,1)}, u32[]{:S(2)}) copy-start(bf16[512,3,128]{2,0,1:T(8,128)(2,1)} %param.6) | copy-start | bytes 1179652
  0.0 29.1 %copy-start = (bf16[512,3,128]{2,0,1:T(8,128)(2,1)S(1)}, bf16[512,3,128]{2,0,1:T(8,128)(2,1)}, u32[]{:S(2)}) copy-start(bf16[512,3,128]{2,0,1:T(8,128)(2,1)} %param.5) | copy-start | bytes 1179652
  0.0 29.2 %copy-start.2 = (bf16[512,3,128]{2,0,1:T(8,128)(2,1)S(1)}, bf16[512,3,128]{2,0,1:T(8,128)(2,1)}, u32[]{:S(2)}) copy-start(bf16[512,3,128]{2,0,1:T(8,128)(2,1)} %param.4) | copy-start | bytes 1179652
  2.6 26.6 %collective-permute-start = (bf16[3,320,128]{2,1,0:T(8,128)(2,1)}, bf16[3,320,128]{2,1,0:T(8,128)(2,1)S(1)}, u32[]{:S(2)}, u32[]{:S(2)}) collective-permute-start(bf16[3,320,128]{2,1,0:T(8,128)(2,1)} %get-tuple-element.26), channel_id=1, source_target_pairs={{0,4},{4,0},{8,12},{12,8},{16,20},{20,16},{24,28},{28,24},{32,36},... | collective-permute-start | bytes 737288 | tf_op jit(solution)/shard_map/ppermute | solution.py:359
  6.2 22.9 %all-to-all-start = ((bf16[64,3,128]{2,1,0:T(4,128)(2,1)}), bf16[64,3,128]{2,1,0:T(4,128)(2,1)S(1)}, u32[]{:S(2)}, u32[]{:S(2)}) async-start(bf16[64,3,128]{2,1,0:T(4,128)(2,1)} %get-tuple-element.25), calls=%async_computation | async-start | bytes 131072 | tf_op jit(solution)/shard_map/all_to_all | solution.py:386
  18.1 14.0 %collective-permute-start.1 = (bf16[3,320,128]{2,1,0:T(8,128)(2,1)}, bf16[3,320,128]{2,1,0:T(8,128)(2,1)S(1)}, u32[]{:S(2)}, u32[]{:S(2)}) collective-permute-start(bf16[3,320,128]{2,1,0:T(8,128)(2,1)} %get-tuple-element.36), channel_id=1, source_target_pairs={{0,252},{4,8},{8,4},{12,16},{16,12},{20,24},{24,20},{28,32},{32,28... | collective-permute-start | bytes 737288 | tf_op jit(solution)/shard_map/ppermute | solution.py:385
  25.2 1.0 %copy-start.3 = (bf16[192,768]{1,0:T(8,128)(2,1)S(1)}, bf16[192,768]{1,0:T(8,128)(2,1)}, u32[]{:S(2)}) copy-start(bf16[192,768]{1,0:T(8,128)(2,1)} %w_ref) | copy-start | bytes 884740
  26.9 12.6 %collective-permute-start.3 = (bf16[192,384]{1,0:T(8,128)(2,1)S(1)}, bf16[192,384]{1,0:T(8,128)(2,1)S(1)}, u32[]{:S(2)}, u32[]{:S(2)}) collective-permute-start(bf16[192,384]{1,0:T(8,128)(2,1)S(1)} %get-tuple-element.40), channel_id=1, source_target_pairs={{0,2},{1,3},{2,0},{3,1},{4,6},{5,7},{6,4},{7,5},{8,10},{9,11},{10,... | collective-permute-start | bytes 442376 | tf_op jit(solution)/shard_map/ppermute | solution.py:359
  33.6 5.9 %collective-permute-start.4 = (bf16[512,128]{1,0:T(8,128)(2,1)S(1)}, bf16[512,128]{1,0:T(8,128)(2,1)S(1)}, u32[]{:S(2)}, u32[]{:S(2)}) collective-permute-start(bf16[512,128]{1,0:T(8,128)(2,1)S(1)} %bitcast.28), channel_id=1, source_target_pairs={{0,2},{1,3},{2,0},{3,1},{4,6},{5,7},{6,4},{7,5},{8,10},{9,11},{10,... | collective-permute-start | bytes 393224 | tf_op jit(solution)/shard_map/ppermute | solution.py:359
  36.4 5.2 %collective-permute-start.5 = (bf16[512,128]{1,0:T(8,128)(2,1)S(1)}, bf16[512,128]{1,0:T(8,128)(2,1)S(1)}, u32[]{:S(2)}, u32[]{:S(2)}) collective-permute-start(bf16[512,128]{1,0:T(8,128)(2,1)S(1)} %bitcast.30), channel_id=1, source_target_pairs={{0,2},{1,3},{2,0},{3,1},{4,6},{5,7},{6,4},{7,5},{8,10},{9,11},{10,... | collective-permute-start | bytes 393224 | tf_op jit(solution)/shard_map/ppermute | solution.py:359
  38.3 6.0 %collective-permute-start.2 = (bf16[512,128]{1,0:T(8,128)(2,1)S(1)}, bf16[512,128]{1,0:T(8,128)(2,1)S(1)}, u32[]{:S(2)}, u32[]{:S(2)}) collective-permute-start(bf16[512,128]{1,0:T(8,128)(2,1)S(1)} %bitcast.32), channel_id=1, source_target_pairs={{0,2},{1,3},{2,0},{3,1},{4,6},{5,7},{6,4},{7,5},{8,10},{9,11},{10,... | collective-permute-start | bytes 393224 | tf_op jit(solution)/shard_map/ppermute | solution.py:359
  44.7 3.5 %collective-permute-start.6 = (bf16[3,512,128]{2,1,0:T(8,128)(2,1)S(1)}, bf16[3,512,128]{2,1,0:T(8,128)(2,1)S(1)}, u32[]{:S(2)}, u32[]{:S(2)}) collective-permute-start(bf16[3,512,128]{2,1,0:T(8,128)(2,1)S(1)} %get-tuple-element.44), channel_id=1, source_target_pairs={{0,1},{1,0},{2,3},{3,2},{4,5},{5,4},{6,7},{7,6},{8,9},{9,8},{10,11... | collective-permute-start | bytes 1179656 | tf_op jit(solution)/shard_map/ppermute | solution.py:359
